TPU v7x, 128 devices: a whole 4x4x4 slice. The times are simulated.
128 devices in a mesh: row: 8 (over y, x_hi), col: 16 (over z, x_lo, core).
Axes of the slice: x: 4 (x_hi: 2, x_lo: 2; x = x_hi * 2 + x_lo), y: 4, z: 4, core: 2. Of those that a mesh axis runs over, the one named last changes fastest.
Arguments:
- amplitudes: float32 [384, 384, 1600], P('row', 'col'), may hold values from -6 to 6
- hole_ladder: float32 [1600, 1600], P('col'), may hold values from -0.15625 to 0.15625
- e_occ: float32 [40], replicated, may hold values from -2 to -0.5
- e_vir: float32 [384], replicated, may hold values from 0.5 to 4
- ladder_ints: float32 [384, 384, 256], P('col'), may hold values from -0.09375 to 0.09375
- pair_group: int32 [820], replicated, may hold values from 0 to 7, as said below
Outputs:
- new_amplitudes: float32 [8, 205, 384, 384], P('row', None, 'col')
- particle_term: float32 [8, 256, 205], P('row', 'col')
Inputs may be any that keep to these rules, and one draw needn't show every extreme that they name: `pair_group`: each pair names its row group; no group holds more than 205 pairs, and one group holds exactly 205.
All inputs are finite; a program needn't handle non-finite values.
Results may differ from a plain program's by a relative error of at most 0.00011.
Values sent between devices are 32-bit elements; how exact they have to be, the bound alone decides.
No kernel may reach another device: no remote copies, remote signals or barrier semaphores. Data moves between devices by JAX's collectives and lax.ppermute only.
A program may use at most 192 MiB of HBM per device.

v0:
```python
import functools

import jax
import jax.numpy as jnp
import numpy as np
from jax import lax
from jax.experimental import pallas as pl
from jax.experimental.pallas import tpu as pltpu
from jax.sharding import PartitionSpec as P

F32 = jnp.float32
BF16 = jnp.bfloat16
BINS = 8
SLOTS = 104
ALL_SLOTS = BINS * SLOTS
SPILL = 20
PAIR_PAD = 896
GROUP_SLOTS = 256
OCC = 40
VMEM_LIMIT = 56 * 1024 * 1024


def split2(x):
    hi = x.astype(BF16)
    return hi, (x - hi.astype(F32)).astype(BF16)


def split3(x):
    hi = x.astype(BF16)
    rest = x - hi.astype(F32)
    mid = rest.astype(BF16)
    return hi, mid, (rest - mid.astype(F32)).astype(BF16)


def dot(a, b):
    return jnp.dot(a, b, preferred_element_type=F32)


def dot_t(a, b):
    return lax.dot_general(a, b, (((1,), (1,)), ((), ())), preferred_element_type=F32)


def iota(shape, dim):
    return lax.broadcasted_iota(jnp.int32, shape, dim)


def prep_kernel(own_ref, group_ref, occ_ref, eocc_ref, w_ref, mirror_out, direct_out, slot_out, group_out, bin_out):
    group = group_ref[...]
    onehot = jnp.where(group == iota((BINS, PAIR_PAD), 0), 1.0, 0.0)
    before = jnp.where(iota((PAIR_PAD, PAIR_PAD), 0) < iota((PAIR_PAD, PAIR_PAD), 1), 1.0, 0.0).astype(BF16)
    rank = jnp.sum(dot(onehot.astype(BF16), before) * onehot, axis=0, keepdims=True)
    valid = jnp.sum(onehot, axis=0, keepdims=True)
    count = jnp.sum(onehot, axis=1, keepdims=True)
    kept = jnp.minimum(count, float(SLOTS))
    spilled = jnp.where(rank >= float(SLOTS), valid, 0.0)
    order = dot(jnp.broadcast_to(spilled, (BINS, PAIR_PAD)).astype(BF16), before)
    total = jnp.sum(spilled, axis=1, keepdims=True)
    free = float(SLOTS) - kept
    short = jnp.minimum(free, float(SPILL))
    fits = jnp.sum(short, axis=0, keepdims=True) >= total
    room = jnp.where(fits, short, free)
    bin_row = iota((BINS, 1), 0)
    first = jnp.zeros((BINS, 1), F32)
    for b in range(BINS - 1):
        first = first + jnp.where(bin_row > b, room[b : b + 1, :], 0.0)
    inside = jnp.where(order >= first, jnp.where(order < first + room, 1.0, 0.0), 0.0)
    is_spilled = spilled > 0.5
    bin_hot = jnp.where(is_spilled, inside, onehot)
    bin_of = jnp.sum(bin_hot * bin_row.astype(F32), axis=0, keepdims=True)
    moved = jnp.sum(inside * (kept - first), axis=0, keepdims=True) + order[0:1, :]
    slot_of = jnp.where(is_spilled, moved, rank)
    place = jnp.where(valid > 0.5, bin_of * float(SLOTS) + slot_of, -1.0)
    own_rank = jnp.where(group == own_ref[0], rank, -1.0)
    stack = jnp.concatenate([place, own_rank, jnp.zeros((6, PAIR_PAD), F32)], axis=0)
    columns = jnp.transpose(stack, (1, 0))
    place_col = columns[:, 0:1].astype(jnp.int32)
    rank_col = columns[:, 1:2].astype(jnp.int32)
    to_slot = jnp.where(place_col == iota((PAIR_PAD, ALL_SLOTS), 1), 1.0, 0.0).astype(BF16)
    slots = dot(occ_ref[...].astype(BF16), to_slot)
    slot_i, slot_j, live = slots[0:1, :], slots[1:2, :], slots[2:3, :]
    occ_row = iota((OCC, 1), 0).astype(F32)
    energy = jnp.sum(
        jnp.where(slot_i == occ_row, eocc_ref[...], 0.0), axis=0, keepdims=True
    ) + jnp.sum(jnp.where(slot_j == occ_row, eocc_ref[...], 0.0), axis=0, keepdims=True)
    slot_out[...] = jnp.concatenate([energy, live, jnp.zeros((6, ALL_SLOTS), F32)], axis=0)
    to_group = jnp.where(rank_col == iota((PAIR_PAD, GROUP_SLOTS), 1), 1.0, 0.0).astype(BF16)
    source = jnp.concatenate([bin_of, slot_of, valid, jnp.zeros((5, PAIR_PAD), F32)], axis=0)
    group_out[...] = dot(source.astype(BF16), to_group).astype(jnp.int32)
    taken = jnp.minimum(jnp.maximum(total - first, 0.0), room)
    bin_cols = jnp.concatenate([count, kept, first, taken, jnp.zeros((BINS, 124), F32)], axis=1)
    bin_out[...] = bin_cols.astype(jnp.int32)

    parts = split3(w_ref[...])
    rows = w_ref.shape[0]
    for left, right, w_out in ((slot_j, slot_i, mirror_out), (slot_i, slot_j, direct_out)):
        wanted = jnp.where(live > 0.5, left * float(OCC) + right, -1.0).astype(jnp.int32)
        w_out[...] = jnp.zeros(w_out.shape, F32)
        for lane in range(0, ALL_SLOTS, 128):
            wide = min(128, ALL_SLOTS - lane)
            pick = jnp.where(
                iota((OCC * OCC, wide), 0) == wanted[:, lane : lane + wide], 1.0, 0.0
            ).astype(BF16)
            w_out[0:rows, lane : lane + wide] = (dot(parts[0], pick) + dot(parts[1], pick)) + dot(
                parts[2], pick
            )


def prep(own, pair_group, e_occ, hole_ladder):
    pairs = pair_group.shape[0]
    first, second = np.triu_indices(OCC)
    occ = np.zeros((8, PAIR_PAD), np.float32)
    occ[0, :pairs], occ[1, :pairs], occ[2, :pairs] = first, second, 1.0
    group = jnp.pad(pair_group, (0, PAIR_PAD - pairs), constant_values=BINS).reshape(1, PAIR_PAD)
    vmem = pl.BlockSpec(memory_space=pltpu.VMEM)
    return pl.pallas_call(
        prep_kernel,
        out_shape=(
            jax.ShapeDtypeStruct((104, ALL_SLOTS), F32),
            jax.ShapeDtypeStruct((104, ALL_SLOTS), F32),
            jax.ShapeDtypeStruct((8, ALL_SLOTS), F32),
            jax.ShapeDtypeStruct((8, GROUP_SLOTS), jnp.int32),
            jax.ShapeDtypeStruct((BINS, 128), jnp.int32),
        ),
        in_specs=[pl.BlockSpec(memory_space=pltpu.SMEM)] + [vmem] * 4,
        out_specs=(vmem,) * 5,
        compiler_params=pltpu.CompilerParams(vmem_limit_bytes=VMEM_LIMIT),
    )(own, group, jnp.asarray(occ), e_occ.reshape(OCC, 1), hole_ladder)


def tile_kernel(t_ref, mirror_hi, mirror_lo, direct_hi, direct_lo):
    for h in range(2):
        for tile in range(5):
            for q in range(8):
                pieces = []
                for e in (2 * q, 2 * q + 1):
                    unit = 5 * tile + e // 3
                    if e < 15 and unit < 24:
                        pieces.append(t_ref[24 * h + unit, 8 * (e % 3) : 8 * (e % 3) + 8, :])
                    else:
                        pieces.append(jnp.zeros((8, 1600), F32))
                hi, lo = split2(jnp.concatenate(pieces, axis=0))
                at = 640 * h + 128 * tile + 16 * q
                mirror_hi[at : at + 16, :] = hi
                mirror_lo[at : at + 16, :] = lo
    for b in range(24):
        hi, lo = split2(t_ref[:, b, :])
        direct_hi[48 * b : 48 * (b + 1), :] = hi
        direct_lo[48 * b : 48 * (b + 1), :] = lo
    direct_hi[1152:1280, :] = jnp.zeros((128, 1600), BF16)
    direct_lo[1152:1280, :] = jnp.zeros((128, 1600), BF16)


def tile_parts(amplitudes):
    vmem = pl.BlockSpec(memory_space=pltpu.VMEM)
    return pl.pallas_call(
        tile_kernel,
        out_shape=(jax.ShapeDtypeStruct((1280, 1600), BF16),) * 4,
        in_specs=[vmem],
        out_specs=(vmem,) * 4,
        compiler_params=pltpu.CompilerParams(vmem_limit_bytes=VMEM_LIMIT),
        cost_estimate=pl.CostEstimate(flops=0, bytes_accessed=60_000_000, transcendentals=0),
    )(amplitudes)


def hole_kernel(mirror, w_ref, t_hi, t_lo, out_ref, wn, wt_hi, wt_lo):
    for s in range(16):
        wn[100 * s : 100 * s + 100, :] = w_ref[104 * s : 104 * s + 100, :]
    for lane in range(0, ALL_SLOTS, 128):
        wide = min(128, ALL_SLOTS - lane)
        hi, lo = split2(jnp.transpose(wn[:, lane : lane + wide], (1, 0)))
        wt_hi[lane : lane + wide, :] = hi
        wt_lo[lane : lane + wide, :] = lo

    for n in range(5):
        right_hi, right_lo = t_hi[256 * n : 256 * (n + 1), :], t_lo[256 * n : 256 * (n + 1), :]
        y = (dot_t(wt_lo[...], right_hi) + dot_t(wt_hi[...], right_lo)) + dot_t(wt_hi[...], right_hi)
        for b in range(BINS):
            rows = slice(SLOTS * b, SLOTS * (b + 1))
            if mirror:
                for u in range(2):
                    h, lane = divmod(2 * n + u, 5)
                    out_ref[b, h, :, 128 * lane : 128 * (lane + 1)] = y[rows, 128 * u : 128 * (u + 1)]
            else:
                wide = 256 if n < 4 else 128
                out_ref[b, :, 256 * n : 256 * n + wide] = y[rows, 0:wide]


def hole_product(mirror, gathered, hi, lo):
    shape = (BINS, 2, SLOTS, 640) if mirror else (BINS, SLOTS, 1152)
    vmem = pl.BlockSpec(memory_space=pltpu.VMEM)
    return pl.pallas_call(
        functools.partial(hole_kernel, mirror),
        out_shape=jax.ShapeDtypeStruct(shape, F32),
        in_specs=[vmem] * 3,
        out_specs=vmem,
        scratch_shapes=[
            pltpu.VMEM((1600, ALL_SLOTS), F32),
            pltpu.VMEM((ALL_SLOTS, 1600), BF16),
            pltpu.VMEM((ALL_SLOTS, 1600), BF16),
        ],
        compiler_params=pltpu.CompilerParams(vmem_limit_bytes=VMEM_LIMIT),
        cost_estimate=pl.CostEstimate(
            flops=2 * 3 * ALL_SLOTS * 1280 * 1600, bytes_accessed=17_000_000, transcendentals=0
        ),
    )(gathered, hi, lo)


def combine_kernel(meta_ref, ed_ref, d_ref, s_ref, eo_ref, ev_ref, ladder_ref, new_ref, seg_ref, part_ref, m_ref, raw, acc):
    step = pl.program_id(0)
    kept, start = meta_ref[0], meta_ref[1]
    energy = eo_ref[:, 0:1] - ev_ref[...]
    live = eo_ref[:, 1:2] > 0.5
    rest = new_ref.shape[0] - SLOTS

    def group(j):
        for u in range(8):
            d = 8 * j + u
            direct = jnp.concatenate([d_ref[r, :, 48 * u : 48 * (u + 1)] for r in range(8)], axis=1)
            lane = 128 * (d // 5) + 24 * (d % 5)
            mirrored = jnp.concatenate([s_ref[c, :, lane : lane + 24] for c in range(16)], axis=1)
            value = jnp.where(live, (direct + mirrored) / (energy - ed_ref[d]), 0.0)
            m_ref[:, 384 * u : 384 * (u + 1)] = value
            raw[:, u, :] = value

    for j in range(3):
        pl.when(step == j)(functools.partial(group, j))

    new_ref[0:SLOTS] = jnp.where(iota((SLOTS, 8, 384), 0) < kept, raw[...], 0.0)
    new_ref[SLOTS:] = jnp.zeros((rest, 8, 384), F32)
    seg_ref[...] = raw[pl.ds(start, SPILL)]

    left_hi, left_lo = split2(m_ref[...])
    right_hi, right_lo = split2(ladder_ref[...].reshape(8 * 384, 256))
    term = (dot(left_lo, right_hi) + dot(left_hi, right_lo)) + dot(left_hi, right_hi)

    @pl.when(step == 0)
    def _():
        acc[...] = jnp.zeros(acc.shape, F32)

    acc[0:SLOTS, :] += term

    @pl.when(step == 2)
    def _():
        part_ref[...] = jnp.transpose(acc[...], (1, 0))


def combine(meta, ed, direct, mirrored, energy, ev, ladder, rows):
    smem = pl.BlockSpec(memory_space=pltpu.SMEM)
    return pl.pallas_call(
        combine_kernel,
        grid=(3,),
        out_shape=(
            jax.ShapeDtypeStruct((rows, 24, 384), F32),
            jax.ShapeDtypeStruct((SPILL, 24, 384), F32),
            jax.ShapeDtypeStruct((256, 128), F32),
        ),
        in_specs=[
            smem,
            smem,
            pl.BlockSpec((8, SLOTS, 384), lambda j: (0, 0, j)),
            pl.BlockSpec((16, SLOTS, 640), lambda j: (0, 0, 0)),
            pl.BlockSpec((SLOTS, 2), lambda j: (0, 0)),
            pl.BlockSpec((1, 384), lambda j: (0, 0)),
            pl.BlockSpec((8, 384, 256), lambda j: (j, 0, 0)),
        ],
        out_specs=(
            pl.BlockSpec((rows, 8, 384), lambda j: (0, j, 0)),
            pl.BlockSpec((SPILL, 8, 384), lambda j: (0, j, 0)),
            pl.BlockSpec((256, 128), lambda j: (0, 0)),
        ),
        scratch_shapes=[
            pltpu.VMEM((SLOTS, 8 * 384), F32),
            pltpu.VMEM((SLOTS, 8, 384), F32),
            pltpu.VMEM((128, 256), F32),
        ],
        compiler_params=pltpu.CompilerParams(vmem_limit_bytes=VMEM_LIMIT),
        cost_estimate=pl.CostEstimate(
            flops=2 * 3 * 128 * 9216 * 256, bytes_accessed=60_000_000, transcendentals=0
        ),
    )(meta, ed, direct, mirrored, energy, ev, ladder)


def place_kernel(table_ref, new_ref, *refs):
    back_refs, out_ref, sem = refs[:BINS], refs[BINS], refs[BINS + 1]
    for b in range(BINS):

        def send(k, carry, b=b):
            row = back_refs[b].at[table_ref[0, b] + k]
            pltpu.make_async_copy(row, out_ref.at[table_ref[1, b] + k], sem).start()
            return carry

        lax.fori_loop(0, table_ref[2, b], send, 0)

    for b in range(BINS):

        def wait(k, carry, b=b):
            pltpu.make_async_copy(back_refs[b].at[k], out_ref.at[k], sem).wait()
            return carry

        lax.fori_loop(0, table_ref[2, b], wait, 0)


def place(table, new, backs):
    hbm = pl.BlockSpec(memory_space=pl.ANY)
    vmem = pl.BlockSpec(memory_space=pltpu.VMEM)
    return pl.pallas_call(
        place_kernel,
        out_shape=jax.ShapeDtypeStruct(new.shape, F32),
        in_specs=[pl.BlockSpec(memory_space=pltpu.SMEM), hbm] + [vmem] * BINS,
        out_specs=hbm,
        scratch_shapes=[pltpu.SemaphoreType.DMA],
        input_output_aliases={1: 0},
        compiler_params=pltpu.CompilerParams(vmem_limit_bytes=VMEM_LIMIT),
    )(table, new, *backs)


def shards(amplitudes, hole_ladder, e_occ, e_vir, ladder_ints, pair_group):
    tile_cols = amplitudes.shape[1]
    capacity = 2 * pair_group.shape[0] // lax.axis_size("row")
    own = lax.axis_index("row")
    col_index = lax.axis_index("col")

    w_mirror, w_direct, slot_table, group_table, bin_table = prep(
        own.reshape(1), pair_group, e_occ, hole_ladder
    )
    w_mirror = lax.all_gather(w_mirror, "col", axis=0, tiled=True)
    w_direct = lax.all_gather(w_direct, "col", axis=0, tiled=True)
    mirror_hi, mirror_lo, direct_hi, direct_lo = tile_parts(amplitudes)
    mirror_src = hole_product(True, w_mirror, mirror_hi, mirror_lo)
    mirrored = lax.all_to_all(mirror_src, "row", 0, 0).reshape(16, SLOTS, 640)
    direct_src = hole_product(False, w_direct, direct_hi, direct_lo)
    mirrored = lax.all_to_all(mirrored, "col", 0, 0)
    direct = lax.all_to_all(direct_src, "row", 0, 0)

    counts, kept, first, taken = (bin_table[:, k] for k in range(4))
    own_count = lax.dynamic_index_in_dim(counts, own, 0, False)
    own_kept = jnp.minimum(own_count, SLOTS)
    start = jnp.minimum(kept, SLOTS - SPILL)
    own_start = lax.dynamic_index_in_dim(start, own, 0, False)
    energy = lax.dynamic_slice(slot_table, (0, own * SLOTS), (2, SLOTS)).T
    local_energy = lax.dynamic_slice_in_dim(e_vir, col_index * tile_cols, tile_cols)
    virtual = e_vir.reshape(1, -1)
    new_rows, segment, partial_value = combine(
        jnp.stack([own_kept, own_start]), local_energy, direct, mirrored, energy, virtual, ladder_ints, capacity
    )

    blocks = lax.all_to_all(partial_value.reshape(16, 16, 128), "col", 0, 0)
    share = jnp.sum(blocks, axis=0)
    shares = lax.all_to_all(jnp.broadcast_to(share, (BINS, 16, 128)), "row", 0, 0)
    live = group_table[2, :capacity]
    from_bin, from_slot = group_table[0, :capacity], group_table[1, :capacity]
    where_from = jnp.where(live > 0, from_bin * 128 + from_slot, -1)
    pick = jnp.arange(BINS * 128, dtype=jnp.int32)[:, None] == where_from[None, :]
    ladder_share = jnp.dot(
        jnp.transpose(shares, (1, 0, 2)).reshape(16, BINS * 128),
        pick.astype(F32),
        precision=lax.Precision.HIGHEST,
        preferred_element_type=F32,
    )

    hot = jnp.argmax(counts).astype(jnp.int32)
    fits = (jnp.sum((counts > SLOTS).astype(jnp.int32)) <= 1) & (jnp.max(taken) <= SPILL)

    def short_way(h, operands):
        segment = operands[0]
        return tuple(
            segment if r == h else lax.ppermute(segment, "row", [(r, h)]) for r in range(BINS)
        )

    def long_way(operands):
        _, direct, mirrored = operands
        whole = jnp.stack([jnp.int32(SLOTS), jnp.int32(0)])
        values, _, _ = combine(
            whole, local_energy, direct, mirrored, energy, virtual, ladder_ints, capacity
        )
        everything = lax.all_gather(values[:SLOTS], "row", axis=0, tiled=True)
        index = jnp.pad((from_bin * SLOTS + from_slot)[SLOTS:], (0, BINS * SPILL + SLOTS - capacity))
        late = everything[index].reshape(BINS, SPILL, 24, 384)
        return tuple(late[b] for b in range(BINS))

    ways = [functools.partial(short_way, h) for h in range(BINS)] + [long_way]
    backs = lax.switch(jnp.where(fits, hot, BINS), ways, (segment, direct, mirrored))
    late_count = own_count - own_kept
    bins = SPILL * jnp.arange(BINS, dtype=jnp.int32)
    short_table = jnp.stack([kept - start, SLOTS + first, jnp.where(own == hot, taken, 0)])
    long_table = jnp.stack([jnp.zeros_like(bins), SLOTS + bins, jnp.clip(late_count - bins, 0, SPILL)])
    new_amps = place(jnp.where(fits, short_table, long_table), new_rows, backs)
    return (new_amps[None], ladder_share[None])


def solution(mesh):
    return jax.shard_map(
        shards,
        mesh=mesh,
        in_specs=(P("row", "col", None), P("col", None), P(), P(), P("col", None, None), P()),
        out_specs=(P("row", None, "col", None), P("row", "col", None)),
        check_vma=False,
    )
```

profile of v0, /device:TPU:8, one launch (start us, length us, event | category | flops | bytes accessed | tf_op | source)
XLA Modules:
  0.0 401.2 jit_solution(18008772271256503034)
XLA Ops:
  8.5 1.3 copy.14.eocc_ref
  9.8 7.9 %shard_map.86 = (f32[104,832]{1,0:T(8,128)}, f32[104,832]{1,0:T(8,128)}, f32[8,832]{1,0:T(8,128)}, s32[8,256]{1,0:T(8,128)}, s32[8,128]{1,0:T(8,128)}) custom-call(s32[1]{0:T(128)} %bitcast.1.own_ref, s32[1,896]{1,0:T(1,128)} %reshape.113.group_ref, f32[8,896]{1,0:T(8,128)} %constant.62.clone.occ_ref, f32[40,1]{1,0:T(8,128)} %copy.14.eocc_ref, f32[100,1600]{1,0:T(8,128)} %w_ref.1), custom_call_target="tpu_custom_call" | custom-call | tf_op jit(solution)/shard_map/pallas_call | solution.py:115
  18.5 33.5 %shard_map.87 = (bf16[1280,1600]{1,0:T(8,128)(2,1)}, bf16[1280,1600]{1,0:T(8,128)(2,1)}, bf16[1280,1600]{1,0:T(8,128)(2,1)}, bf16[1280,1600]{1,0:T(8,128)(2,1)}) custom-call(f32[48,24,1600]{2,1,0:T(8,128)} %t_ref.1), custom_call_target="tpu_custom_call" | custom-call | bytes 60000000 | tf_op jit(solution)/shard_map/pallas_call | solution.py:155
  52.0 9.6 %all-gather.6.cloned.1.call-done.w_ref = f32[1664,832]{1,0:T(8,128)} async-done(((f32[104,832]{1,0:T(8,128)}), f32[1664,832]{1,0:T(8,128)}) %all-gather.6.cloned.1.call-update) | async-done | bytes 5537808 | tf_op jit(solution)/shard_map/all_gather | solution.py:327
  61.6 19.7 %shard_map.88 = f32[8,104,1152]{2,1,0:T(8,128)} custom-call(f32[1664,832]{1,0:T(8,128)} %all-gather.6.cloned.1.call-done.w_ref, bf16[1280,1600]{1,0:T(8,128)(2,1)} %get-tuple-element.61.t_hi, bf16[1280,1600]{1,0:T(8,128)(2,1)} %get-tuple-element.62.t_lo), custom_call_target="tpu_custom_call" | custom-call | flops 10223616000 | bytes 17000000 | tf_op jit(solution)/shard_map/pallas_call | solution.py:191
  81.3 6.9 %all-to-all-start = ((f32[8,104,1152]{2,1,0:T(8,128)}), f32[8,104,1152]{2,1,0:T(8,128)}, u32[]{:S(2)}, u32[]{:S(2)}) async-start(f32[8,104,1152]{2,1,0:T(8,128)} %shard_map.88), calls=%async_computation | async-start | bytes 7667712 | tf_op jit(solution)/shard_map/all_to_all | solution.py:333
  88.2 30.6 %all-gather.8.cloned.1.call-done.w_ref = f32[1664,832]{1,0:T(8,128)} async-done(((f32[104,832]{1,0:T(8,128)}), f32[1664,832]{1,0:T(8,128)}) %all-gather.8.cloned.1.call-update) | async-done | bytes 5537808 | tf_op jit(solution)/shard_map/all_gather | solution.py:326
  118.9 19.7 %shard_map.89 = f32[8,2,104,640]{3,2,1,0:T(8,128)} custom-call(f32[1664,832]{1,0:T(8,128)} %all-gather.8.cloned.1.call-done.w_ref, bf16[1280,1600]{1,0:T(8,128)(2,1)} %get-tuple-element.64.t_hi, bf16[1280,1600]{1,0:T(8,128)(2,1)} %get-tuple-element.65.t_lo), custom_call_target="tpu_custom_call" | custom-call | flops 10223616000 | bytes 17000000 | tf_op jit(solution)/shard_map/pallas_call | solution.py:191
  138.6 7.9 %all-to-all-done.d_ref = f32[8,104,1152]{2,1,0:T(8,128)} async-done(((f32[8,104,1152]{2,1,0:T(8,128)}), f32[8,104,1152]{2,1,0:T(8,128)}, u32[]{:S(2)}, u32[]{:S(2)}) %all-to-all-start) | async-done | bytes 3833888 | tf_op jit(solution)/shard_map/all_to_all | solution.py:333
  146.5 56.9 %all_to_all.25 = f32[8,2,104,640]{3,2,1,0:T(8,128)} all-to-all(f32[8,2,104,640]{3,2,1,0:T(8,128)} %shard_map.89), channel_id=1, replica_groups=mesh['row'=8,'col'=16] {'row'}, dimensions={0} | all-to-all | bytes 8519680 | tf_op jit(solution)/shard_map/all_to_all | solution.py:330
  203.4 5.0 %all-to-all-start.2 = ((f32[16,104,640]{2,1,0:T(8,128)}), f32[16,104,640]{2,1,0:T(8,128)}, u32[]{:S(2)}, u32[]{:S(2)}) async-start(f32[16,104,640]{2,1,0:T(8,128)} %bitcast.27), calls=%async_computation.2 | async-start | bytes 8519680 | tf_op jit(solution)/shard_map/all_to_all | solution.py:332
  208.5 0.7 slice_reduce_fusion.1
  209.2 0.7 iota_reduce_fusion
  212.1 1.3 pad_add_fusion.meta_ref
  213.4 0.8 compare_select_fusion.1
  214.2 45.3 %all-to-all-done.2.s_ref = f32[16,104,640]{2,1,0:T(8,128)} async-done(((f32[16,104,640]{2,1,0:T(8,128)}), f32[16,104,640]{2,1,0:T(8,128)}, u32[]{:S(2)}, u32[]{:S(2)}) %all-to-all-start.2) | async-done | bytes 4259872 | tf_op jit(solution)/shard_map/all_to_all | solution.py:332
  259.5 18.0 %shard_map.90 = (f32[205,24,384]{2,1,0:T(8,128)}, f32[20,24,384]{2,1,0:T(8,128)S(1)}, f32[256,128]{1,0:T(8,128)}) custom-call(s32[2]{0:T(128)} %pad_add_fusion.meta_ref, f32[24]{0:T(128)S(1)} %dynamic_slice.18.ed_ref, f32[8,104,1152]{2,1,0:T(8,128)} %all-to-all-done.d_ref, f32[16,104,640]{2,1,0:T(8,128)} %all-to-all-done.2.s_ref, ...), custom_call_target="tpu_custom_call" | custom-call | flops 1811939328 | bytes 60000000 | tf_op jit(solution)/shard_map/pallas_call | solution.py:249
  277.5 3.5 all-to-all-start.3
  284.1 3.6 all-to-all-done.3
  288.4 4.6 %all-to-all-start.4 = ((f32[8,16,128]{2,1,0:T(8,128)}), f32[8,16,128]{2,1,0:T(8,128)S(1)}, u32[]{:S(2)}, u32[]{:S(2)}) async-start(f32[8,16,128]{2,1,0:T(8,128)} %broadcast_in_dim.27), calls=%async_computation.4 | async-start | bytes 131072 | tf_op jit(solution)/shard_map/all_to_all | solution.py:349
  293.6 96.5 %conditional.1 = (f32[20,24,384]{2,1,0:T(8,128)}, f32[20,24,384]{2,1,0:T(8,128)}, f32[20,24,384]{2,1,0:T(8,128)}, f32[20,24,384]{2,1,0:T(8,128)}, f32[20,24,384]...) conditional(s32[]{:T(128)} %clamp.11, ...), branch_computations={%region_3.4_spmd, %region_4.5_spmd, %region_5.6_spmd, %region_6.7_... | conditional | flops 1811941120 | bytes 194782528 | solution.py:382
  293.8 7.7 %collective-permute-start.34 = (f32[20,24,384]{2,1,0:T(8,128)S(1)}, f32[20,24,384]{2,1,0:T(8,128)}, u32[]{:S(2)}, u32[]{:S(2)}) collective-permute-start(f32[20,24,384]{2,1,0:T(8,128)S(1)} %param.4), channel_id=1, source_target_pairs={{112,64},{113,65},{114,66},{115,67},{116,68},{117,69},{118,70},{11... | collective-permute-start | bytes 2211848 | tf_op jit(solution)/shard_map/cond/branch_4_fun/ppermute | solution.py:367
  301.5 10.9 %collective-permute-start.33 = (f32[20,24,384]{2,1,0:T(8,128)S(1)}, f32[20,24,384]{2,1,0:T(8,128)}, u32[]{:S(2)}, u32[]{:S(2)}) collective-permute-start(f32[20,24,384]{2,1,0:T(8,128)S(1)} %param.4), channel_id=1, source_target_pairs={{96,64},{97,65},{98,66},{99,67},{100,68},{101,69},{102,70},{103,71... | collective-permute-start | bytes 2211848 | tf_op jit(solution)/shard_map/cond/branch_4_fun/ppermute | solution.py:367
  312.4 10.4 %collective-permute-start.32 = (f32[20,24,384]{2,1,0:T(8,128)S(1)}, f32[20,24,384]{2,1,0:T(8,128)}, u32[]{:S(2)}, u32[]{:S(2)}) collective-permute-start(f32[20,24,384]{2,1,0:T(8,128)S(1)} %param.4), channel_id=1, source_target_pairs={{80,64},{81,65},{82,66},{83,67},{84,68},{85,69},{86,70},{87,71},{8... | collective-permute-start | bytes 2211848 | tf_op jit(solution)/shard_map/cond/branch_4_fun/ppermute | solution.py:367
  322.8 1.5 collective-permute-start.31
  324.3 3.1 collective-permute-start.30
  327.5 1.5 collective-permute-start.29
  329.0 1.5 collective-permute-start.28
  330.6 0.9 copy.58
  331.4 58.6 %collective-permute-done.30 = f32[20,24,384]{2,1,0:T(8,128)} collective-permute-done((f32[20,24,384]{2,1,0:T(8,128)S(1)}, f32[20,24,384]{2,1,0:T(8,128)}, u32[]{:S(2)}, u32[]{:S(2)}) %collective-permute-start.30) | collective-permute-done | bytes 737312 | tf_op jit(solution)/shard_map/cond/branch_4_fun/ppermute | solution.py:367
  390.1 2.8 shard_map.91
  392.9 1.0 convolution_bitcast_fusion
  (32 shorter events, 5.0 us)
Async XLA Ops:
  7.2 54.5 %all-gather.6.cloned.1.call-start = ((), (), s32[]{:S(2)}) async-start(), calls=%async_computation.6 | async-start | bytes 6336512 | tf_op jit(solution)/shard_map/all_gather | solution.py:327
  17.8 101.1 %all-gather.8.cloned.1.call-start = ((), (), s32[]{:S(2)}) async-start(), calls=%async_computation.7 | async-start | bytes 6336512 | tf_op jit(solution)/shard_map/all_gather | solution.py:326
  81.3 65.2 %all-to-all-start = ((f32[8,104,1152]{2,1,0:T(8,128)}), f32[8,104,1152]{2,1,0:T(8,128)}, u32[]{:S(2)}, u32[]{:S(2)}) async-start(f32[8,104,1152]{2,1,0:T(8,128)} %shard_map.88), calls=%async_computation | async-start | bytes 7667712 | tf_op jit(solution)/shard_map/all_to_all | solution.py:333
  203.4 5.0 %copy-start.2 = (f32[384]{0:T(512)S(1)}, f32[384]{0:T(512)}, u32[]{:S(2)}) copy-start(f32[384]{0:T(512)} %param.19) | copy-start | bytes 4612
  203.4 5.1 %copy-start = (s32[8,128]{1,0:T(8,128)S(1)}, s32[8,128]{1,0:T(8,128)}, u32[]{:S(2)}) copy-start(s32[8,128]{1,0:T(8,128)} %get-tuple-element.58) | copy-start | bytes 12292
  203.4 8.5 %copy-start.1 = (f32[8,832]{1,0:T(8,128)S(1)}, f32[8,832]{1,0:T(8,128)}, u32[]{:S(2)}) copy-start(f32[8,832]{1,0:T(8,128)} %get-tuple-element.66) | copy-start | bytes 79876
  203.4 56.1 %all-to-all-start.2 = ((f32[16,104,640]{2,1,0:T(8,128)}), f32[16,104,640]{2,1,0:T(8,128)}, u32[]{:S(2)}, u32[]{:S(2)}) async-start(f32[16,104,640]{2,1,0:T(8,128)} %bitcast.27), calls=%async_computation.2 | async-start | bytes 8519680 | tf_op jit(solution)/shard_map/all_to_all | solution.py:332
  277.5 10.2 %all-to-all-start.3 = ((f32[16,16,128]{2,1,0:T(8,128)}), f32[16,16,128]{2,1,0:T(8,128)S(1)}, u32[]{:S(2)}, u32[]{:S(2)}) async-start(f32[16,16,128]{2,1,0:T(8,128)} %bitcast.29), calls=%async_computation.3 | async-start | bytes 262144 | tf_op jit(solution)/shard_map/all_to_all | solution.py:347
  288.4 104.5 %all-to-all-start.4 = ((f32[8,16,128]{2,1,0:T(8,128)}), f32[8,16,128]{2,1,0:T(8,128)S(1)}, u32[]{:S(2)}, u32[]{:S(2)}) async-start(f32[8,16,128]{2,1,0:T(8,128)} %broadcast_in_dim.27), calls=%async_computation.4 | async-start | bytes 131072 | tf_op jit(solution)/shard_map/all_to_all | solution.py:349
  293.8 33.7 %collective-permute-start.34 = (f32[20,24,384]{2,1,0:T(8,128)S(1)}, f32[20,24,384]{2,1,0:T(8,128)}, u32[]{:S(2)}, u32[]{:S(2)}) collective-permute-start(f32[20,24,384]{2,1,0:T(8,128)S(1)} %param.4), channel_id=1, source_target_pairs={{112,64},{113,65},{114,66},{115,67},{116,68},{117,69},{118,70},{11... | collective-permute-start | bytes 2211848 | tf_op jit(solution)/shard_map/cond/branch_4_fun/ppermute | solution.py:367
  301.5 27.5 %collective-permute-start.33 = (f32[20,24,384]{2,1,0:T(8,128)S(1)}, f32[20,24,384]{2,1,0:T(8,128)}, u32[]{:S(2)}, u32[]{:S(2)}) collective-permute-start(f32[20,24,384]{2,1,0:T(8,128)S(1)} %param.4), channel_id=1, source_target_pairs={{96,64},{97,65},{98,66},{99,67},{100,68},{101,69},{102,70},{103,71... | collective-permute-start | bytes 2211848 | tf_op jit(solution)/shard_map/cond/branch_4_fun/ppermute | solution.py:367
  312.4 19.0 %collective-permute-start.32 = (f32[20,24,384]{2,1,0:T(8,128)S(1)}, f32[20,24,384]{2,1,0:T(8,128)}, u32[]{:S(2)}, u32[]{:S(2)}) collective-permute-start(f32[20,24,384]{2,1,0:T(8,128)S(1)} %param.4), channel_id=1, source_target_pairs={{80,64},{81,65},{82,66},{83,67},{84,68},{85,69},{86,70},{87,71},{8... | collective-permute-start | bytes 2211848 | tf_op jit(solution)/shard_map/cond/branch_4_fun/ppermute | solution.py:367
  322.8 8.6 %collective-permute-start.31 = (f32[20,24,384]{2,1,0:T(8,128)S(1)}, f32[20,24,384]{2,1,0:T(8,128)}, u32[]{:S(2)}, u32[]{:S(2)}) collective-permute-start(f32[20,24,384]{2,1,0:T(8,128)S(1)} %param.4), channel_id=1, source_target_pairs={{48,64},{49,65},{50,66},{51,67},{52,68},{53,69},{54,70},{55,71},{5... | collective-permute-start | bytes 2211848 | tf_op jit(solution)/shard_map/cond/branch_4_fun/ppermute | solution.py:367
  324.3 65.7 %collective-permute-start.30 = (f32[20,24,384]{2,1,0:T(8,128)S(1)}, f32[20,24,384]{2,1,0:T(8,128)}, u32[]{:S(2)}, u32[]{:S(2)}) collective-permute-start(f32[20,24,384]{2,1,0:T(8,128)S(1)} %param.4), channel_id=1, source_target_pairs={{32,64},{33,65},{34,66},{35,67},{36,68},{37,69},{38,70},{39,71},{4... | collective-permute-start | bytes 2211848 | tf_op jit(solution)/shard_map/cond/branch_4_fun/ppermute | solution.py:367
  327.5 62.6 %collective-permute-start.29 = (f32[20,24,384]{2,1,0:T(8,128)S(1)}, f32[20,24,384]{2,1,0:T(8,128)}, u32[]{:S(2)}, u32[]{:S(2)}) collective-permute-start(f32[20,24,384]{2,1,0:T(8,128)S(1)} %param.4), channel_id=1, source_target_pairs={{16,64},{17,65},{18,66},{19,67},{20,68},{21,69},{22,70},{23,71},{2... | collective-permute-start | bytes 2211848 | tf_op jit(solution)/shard_map/cond/branch_4_fun/ppermute | solution.py:367
  329.0 61.0 %collective-permute-start.28 = (f32[20,24,384]{2,1,0:T(8,128)S(1)}, f32[20,24,384]{2,1,0:T(8,128)}, u32[]{:S(2)}, u32[]{:S(2)}) collective-permute-start(f32[20,24,384]{2,1,0:T(8,128)S(1)} %param.4), channel_id=1, source_target_pairs={{0,64},{1,65},{2,66},{3,67},{4,68},{5,69},{6,70},{7,71},{8,72},{9,... | collective-permute-start | bytes 2211848 | tf_op jit(solution)/shard_map/cond/branch_4_fun/ppermute | solution.py:367
Sparse Core Ops, SparseCore 0:
  17.9 43.6 all-gather.5
  63.3 55.4 all-gather.7
where the time goes:
time: 401 us
  waiting for transfers between devices  156 us (39%)
  Pallas kernels  102 us (25%)
  starting transfers between devices  57.1 us (14%)
  blocking collectives  56.9 us (14%)
  between operations  18.3 us (5%)
  other arithmetic  4.96 us (1%)
  local copies, waits for them, and re-layouts  4.95 us (1%)
    ppermute x7, waiting for transfers between devices, short_way(): lax.ppermute(segment, 'row', [(r, h)])  58.6 us
    all_to_all x1, blocking collectives, shards(): mirrored = lax.all_to_all(mirror_src, 'row', 0, 0).reshape(16, SLOTS, 640)  56.9 us
    all_to_all x1, waiting for transfers between devices, shards(): mirrored = lax.all_to_all(mirrored, 'col', 0, 0)  45.3 us
    pallas_call x2, Pallas kernels, hole_product(): pl.pallas_call(functools.partial(hole_kernel, mirror), out_shape=jax.Shap...  39.4 us
    ppermute x7, starting transfers between devices, short_way(): lax.ppermute(segment, 'row', [(r, h)])  36.7 us
    pallas_call x1, Pallas kernels, tile_parts(): pl.pallas_call(tile_kernel, out_shape=(jax.ShapeDtypeStruct((1280, 1600),...  33.5 us
    all_gather x1, waiting for transfers between devices, shards(): w_mirror = lax.all_gather(w_mirror, 'col', axis=0, tiled=True)  30.6 us
    pallas_call x1, Pallas kernels, combine(): pl.pallas_call(combine_kernel, grid=(3,), out_shape=(jax.ShapeDtypeStruct...  18 us
  transfers between devices with their start and end apart: 13, of which 6 were waited for; matrix products, arithmetic and copies ran while one was open for 2% of the time, Pallas kernels for 19%

commit v1 on v0

v1 whole, which is shorter than its diff:
```python
import functools

import jax
import jax.numpy as jnp
import numpy as np
from jax import lax
from jax.experimental import pallas as pl
from jax.experimental.pallas import tpu as pltpu
from jax.sharding import PartitionSpec as P

F32 = jnp.float32
BF16 = jnp.bfloat16
BINS = 8
SLOTS = 104
HEAD = 72
TAIL = SLOTS - HEAD
ALL_SLOTS = BINS * SLOTS
SPILL = 18
PAIR_PAD = 896
GROUP_SLOTS = 256
OCC = 40
VMEM_LIMIT = 56 * 1024 * 1024


def split2(x):
    hi = x.astype(BF16)
    return hi, (x - hi.astype(F32)).astype(BF16)


def split3(x):
    hi = x.astype(BF16)
    rest = x - hi.astype(F32)
    mid = rest.astype(BF16)
    return hi, mid, (rest - mid.astype(F32)).astype(BF16)


def dot(a, b):
    return jnp.dot(a, b, preferred_element_type=F32)


def dot_t(a, b):
    return lax.dot_general(a, b, (((1,), (1,)), ((), ())), preferred_element_type=F32)


def iota(shape, dim):
    return lax.broadcasted_iota(jnp.int32, shape, dim)


def prep_kernel(own_ref, group_ref, occ_ref, eocc_ref, w_ref, w_direct, w_mirror, slot_out, group_out, bin_out):
    group = group_ref[...]
    onehot = jnp.where(group == iota((BINS, PAIR_PAD), 0), 1.0, 0.0)
    before = jnp.where(iota((PAIR_PAD, PAIR_PAD), 0) < iota((PAIR_PAD, PAIR_PAD), 1), 1.0, 0.0).astype(BF16)
    rank = jnp.sum(dot(onehot.astype(BF16), before) * onehot, axis=0, keepdims=True)
    valid = jnp.sum(onehot, axis=0, keepdims=True)
    count = jnp.sum(onehot, axis=1, keepdims=True)
    kept = jnp.minimum(count, float(SLOTS))
    spilled = jnp.where(rank >= float(SLOTS), valid, 0.0)
    order = dot(jnp.broadcast_to(spilled, (BINS, PAIR_PAD)).astype(BF16), before)
    total = jnp.sum(spilled, axis=1, keepdims=True)
    free = float(SLOTS) - kept
    short = jnp.minimum(free, float(SPILL))
    fits = jnp.sum(short, axis=0, keepdims=True) >= total
    room = jnp.where(fits, short, free)
    bin_row = iota((BINS, 1), 0)
    first = jnp.zeros((BINS, 1), F32)
    for b in range(BINS - 1):
        first = first + jnp.where(bin_row > b, room[b : b + 1, :], 0.0)
    inside = jnp.where(order >= first, jnp.where(order < first + room, 1.0, 0.0), 0.0)
    is_spilled = spilled > 0.5
    bin_hot = jnp.where(is_spilled, inside, onehot)
    bin_of = jnp.sum(bin_hot * bin_row.astype(F32), axis=0, keepdims=True)
    moved = jnp.sum(inside * (kept - first), axis=0, keepdims=True) + order[0:1, :]
    slot_of = jnp.where(is_spilled, moved, rank)
    in_order = bin_of * float(SLOTS) + slot_of
    tail_first = jnp.where(
        slot_of >= float(HEAD),
        bin_of * float(TAIL) + slot_of - float(HEAD),
        bin_of * float(HEAD) + slot_of + float(BINS * TAIL),
    )
    places = [jnp.where(valid > 0.5, place, -1.0) for place in (in_order, tail_first)]
    own_rank = jnp.where(group == own_ref[0], rank, -1.0)
    stack = jnp.concatenate(places + [own_rank, jnp.zeros((5, PAIR_PAD), F32)], axis=0)
    columns = jnp.transpose(stack, (1, 0)).astype(jnp.int32)
    to_group = jnp.where(columns[:, 2:3] == iota((PAIR_PAD, GROUP_SLOTS), 1), 1.0, 0.0).astype(BF16)
    source = jnp.concatenate([bin_of, slot_of, valid, jnp.zeros((5, PAIR_PAD), F32)], axis=0)
    group_out[...] = dot(source.astype(BF16), to_group).astype(jnp.int32)
    taken = jnp.minimum(jnp.maximum(total - first, 0.0), room)
    bin_cols = jnp.concatenate([count, kept, first, taken, jnp.zeros((BINS, 124), F32)], axis=1)
    bin_out[...] = bin_cols.astype(jnp.int32)

    occ_row = iota((OCC, 1), 0).astype(F32)
    parts = split3(w_ref[...])
    rows = w_ref.shape[0]
    for k, w_out in enumerate((w_direct, w_mirror)):
        to_slot = jnp.where(columns[:, k : k + 1] == iota((PAIR_PAD, ALL_SLOTS), 1), 1.0, 0.0).astype(BF16)
        slots = dot(occ_ref[...].astype(BF16), to_slot)
        slot_i, slot_j, live = slots[0:1, :], slots[1:2, :], slots[2:3, :]
        if k == 0:
            wanted = slot_i * float(OCC) + slot_j
        else:
            wanted = slot_j * float(OCC) + slot_i
            energy = jnp.sum(
                jnp.where(slot_i == occ_row, eocc_ref[...], 0.0), axis=0, keepdims=True
            ) + jnp.sum(jnp.where(slot_j == occ_row, eocc_ref[...], 0.0), axis=0, keepdims=True)
            slot_out[...] = jnp.concatenate([energy, live, jnp.zeros((6, ALL_SLOTS), F32)], axis=0)
        wanted = jnp.where(live > 0.5, wanted, -1.0).astype(jnp.int32)
        w_out[...] = jnp.zeros(w_out.shape, F32)
        for lane in range(0, ALL_SLOTS, 128):
            wide = min(128, ALL_SLOTS - lane)
            pick = jnp.where(
                iota((OCC * OCC, wide), 0) == wanted[:, lane : lane + wide], 1.0, 0.0
            ).astype(BF16)
            w_out[0:rows, lane : lane + wide] = (dot(parts[0], pick) + dot(parts[1], pick)) + dot(
                parts[2], pick
            )


def prep(own, pair_group, e_occ, hole_ladder):
    pairs = pair_group.shape[0]
    first, second = np.triu_indices(OCC)
    occ = np.zeros((8, PAIR_PAD), np.float32)
    occ[0, :pairs], occ[1, :pairs], occ[2, :pairs] = first, second, 1.0
    group = jnp.pad(pair_group, (0, PAIR_PAD - pairs), constant_values=BINS).reshape(1, PAIR_PAD)
    vmem = pl.BlockSpec(memory_space=pltpu.VMEM)
    return pl.pallas_call(
        prep_kernel,
        out_shape=(
            jax.ShapeDtypeStruct((104, ALL_SLOTS), F32),
            jax.ShapeDtypeStruct((104, ALL_SLOTS), F32),
            jax.ShapeDtypeStruct((8, ALL_SLOTS), F32),
            jax.ShapeDtypeStruct((8, GROUP_SLOTS), jnp.int32),
            jax.ShapeDtypeStruct((BINS, 128), jnp.int32),
        ),
        in_specs=[pl.BlockSpec(memory_space=pltpu.SMEM)] + [vmem] * 4,
        out_specs=(vmem,) * 5,
        compiler_params=pltpu.CompilerParams(vmem_limit_bytes=VMEM_LIMIT),
    )(own, group, jnp.asarray(occ), e_occ.reshape(OCC, 1), hole_ladder)


def tile_kernel(t_ref, mirror_hi, mirror_lo, direct_hi, direct_lo):
    for h in range(2):
        for tile in range(5):
            for q in range(8):
                pieces = []
                for e in (2 * q, 2 * q + 1):
                    unit = 5 * tile + e // 3
                    if e < 15 and unit < 24:
                        pieces.append(t_ref[24 * h + unit, 8 * (e % 3) : 8 * (e % 3) + 8, :])
                    else:
                        pieces.append(jnp.zeros((8, 1600), F32))
                hi, lo = split2(jnp.concatenate(pieces, axis=0))
                at = 640 * h + 128 * tile + 16 * q
                mirror_hi[at : at + 16, :] = hi
                mirror_lo[at : at + 16, :] = lo
    for b in range(24):
        hi, lo = split2(t_ref[:, b, :])
        direct_hi[48 * b : 48 * (b + 1), :] = hi
        direct_lo[48 * b : 48 * (b + 1), :] = lo
    direct_hi[1152:1280, :] = jnp.zeros((128, 1600), BF16)
    direct_lo[1152:1280, :] = jnp.zeros((128, 1600), BF16)


def tile_parts(amplitudes):
    vmem = pl.BlockSpec(memory_space=pltpu.VMEM)
    return pl.pallas_call(
        tile_kernel,
        out_shape=(jax.ShapeDtypeStruct((1280, 1600), BF16),) * 4,
        in_specs=[vmem],
        out_specs=(vmem,) * 4,
        compiler_params=pltpu.CompilerParams(vmem_limit_bytes=VMEM_LIMIT),
        cost_estimate=pl.CostEstimate(flops=0, bytes_accessed=60_000_000, transcendentals=0),
    )(amplitudes)


def hole_kernel(mirror, w_ref, t_hi, t_lo, *refs):
    out_refs, (wn, wt_hi, wt_lo) = refs[:-3], refs[-3:]
    for s in range(16):
        wn[100 * s : 100 * s + 100, :] = w_ref[104 * s : 104 * s + 100, :]
    for lane in range(0, ALL_SLOTS, 128):
        wide = min(128, ALL_SLOTS - lane)
        hi, lo = split2(jnp.transpose(wn[:, lane : lane + wide], (1, 0)))
        wt_hi[lane : lane + wide, :] = hi
        wt_lo[lane : lane + wide, :] = lo

    for n in range(5):
        right_hi, right_lo = t_hi[256 * n : 256 * (n + 1), :], t_lo[256 * n : 256 * (n + 1), :]
        y = (dot_t(wt_lo[...], right_hi) + dot_t(wt_hi[...], right_lo)) + dot_t(wt_hi[...], right_hi)
        if mirror:
            for u in range(2):
                h, lane = divmod(2 * n + u, 5)
                first = 0
                for out_ref, size in zip(out_refs, (TAIL, HEAD)):
                    for b in range(BINS):
                        out_ref[b, h, :, 128 * lane : 128 * (lane + 1)] = y[
                            first : first + size, 128 * u : 128 * (u + 1)
                        ]
                        first += size
        else:
            wide = 256 if n < 4 else 128
            for b in range(BINS):
                out_refs[0][b, :, 256 * n : 256 * n + wide] = y[SLOTS * b : SLOTS * (b + 1), 0:wide]


def hole_product(mirror, gathered, hi, lo):
    if mirror:
        shapes = [(BINS, 2, TAIL, 640), (BINS, 2, HEAD, 640)]
    else:
        shapes = [(BINS, SLOTS, 1152)]
    vmem = pl.BlockSpec(memory_space=pltpu.VMEM)
    return pl.pallas_call(
        functools.partial(hole_kernel, mirror),
        out_shape=tuple(jax.ShapeDtypeStruct(shape, F32) for shape in shapes),
        in_specs=[vmem] * 3,
        out_specs=(vmem,) * len(shapes),
        scratch_shapes=[
            pltpu.VMEM((1600, ALL_SLOTS), F32),
            pltpu.VMEM((ALL_SLOTS, 1600), BF16),
            pltpu.VMEM((ALL_SLOTS, 1600), BF16),
        ],
        compiler_params=pltpu.CompilerParams(vmem_limit_bytes=VMEM_LIMIT),
        cost_estimate=pl.CostEstimate(
            flops=2 * 3 * ALL_SLOTS * 1280 * 1600, bytes_accessed=17_000_000, transcendentals=0
        ),
    )(gathered, hi, lo)


def combine_kernel(head, size, *refs):
    if head:
        meta_ref, ed_ref, d_ref, s_ref, eo_ref, ev_ref, ladder_ref, tail_ref, more_ref = refs[:9]
        new_ref, part_ref, m_ref, raw, acc = refs[9:]
    else:
        ed_ref, d_ref, s_ref, eo_ref, ev_ref, ladder_ref = refs[:6]
        raw, part_ref, m_ref, acc = refs[6:]
    step = pl.program_id(0)
    energy = eo_ref[:, 0:1] - ev_ref[...]
    live = eo_ref[:, 1:2] > 0.5
    rows = slice(0, size) if head else slice(SLOTS - size, SLOTS)

    def group(j):
        for u in range(8):
            d = 8 * j + u
            direct = jnp.concatenate([d_ref[r, rows, 48 * u : 48 * (u + 1)] for r in range(8)], axis=1)
            lane = 128 * (d // 5) + 24 * (d % 5)
            mirrored = jnp.concatenate([s_ref[c, :, lane : lane + 24] for c in range(16)], axis=1)
            value = jnp.where(live, (direct + mirrored) / (energy - ed_ref[d]), 0.0)
            m_ref[:, 384 * u : 384 * (u + 1)] = value
            raw[:, u, :] = value

    for j in range(3):
        pl.when(step == j)(functools.partial(group, j))

    if head:
        kept = meta_ref[0]
        new_ref[0:size] = jnp.where(iota((size, 8, 384), 0) < kept, raw[...], 0.0)
        tail = iota((SLOTS - size, 8, 384), 0) + size
        new_ref[size:SLOTS] = jnp.where(tail < kept, tail_ref[...], 0.0)
        new_ref[SLOTS:] = jnp.zeros((new_ref.shape[0] - SLOTS, 8, 384), F32)

    left_hi, left_lo = split2(m_ref[...])
    right_hi, right_lo = split2(ladder_ref[...].reshape(8 * 384, 256))
    term = (dot(left_lo, right_hi) + dot(left_hi, right_lo)) + dot(left_hi, right_hi)

    @pl.when(step == 0)
    def _():
        acc[...] = jnp.zeros(acc.shape, F32)
        if head:
            acc[size:SLOTS, :] = more_ref[...]

    acc[0:size, :] += term

    @pl.when(step == 2)
    def _():
        part_ref[...] = jnp.transpose(acc[...], (1, 0)) if head else acc[...]


def combine(size, ed, direct, mirrored, energy, ev, ladder, head=None, rows=0):
    smem = pl.BlockSpec(memory_space=pltpu.SMEM)
    in_specs = [
        smem,
        pl.BlockSpec((8, SLOTS, 384), lambda j: (0, 0, j)),
        pl.BlockSpec((16, size, 640), lambda j: (0, 0, 0)),
        pl.BlockSpec((size, 2), lambda j: (0, 0)),
        pl.BlockSpec((1, 384), lambda j: (0, 0)),
        pl.BlockSpec((8, 384, 256), lambda j: (j, 0, 0)),
    ]
    operands = [ed, direct, mirrored, energy, ev, ladder]
    scratch = [pltpu.VMEM((size, 8 * 384), F32)]
    if head is None:
        out_shape = (jax.ShapeDtypeStruct((size, 24, 384), F32), jax.ShapeDtypeStruct((size, 256), F32))
        out_specs = (
            pl.BlockSpec((size, 8, 384), lambda j: (0, j, 0)),
            pl.BlockSpec((size, 256), lambda j: (0, 0)),
        )
        scratch += [pltpu.VMEM((size, 256), F32)]
    else:
        meta, tail, more = head
        operands = [meta] + operands + [tail, more]
        in_specs = [smem] + in_specs + [
            pl.BlockSpec((SLOTS - size, 8, 384), lambda j: (0, j, 0)),
            pl.BlockSpec((SLOTS - size, 256), lambda j: (0, 0)),
        ]
        out_shape = (jax.ShapeDtypeStruct((rows, 24, 384), F32), jax.ShapeDtypeStruct((256, 128), F32))
        out_specs = (
            pl.BlockSpec((rows, 8, 384), lambda j: (0, j, 0)),
            pl.BlockSpec((256, 128), lambda j: (0, 0)),
        )
        scratch += [pltpu.VMEM((size, 8, 384), F32), pltpu.VMEM((128, 256), F32)]
    return pl.pallas_call(
        functools.partial(combine_kernel, head is not None, size),
        grid=(3,),
        out_shape=out_shape,
        in_specs=in_specs,
        out_specs=out_specs,
        scratch_shapes=scratch,
        compiler_params=pltpu.CompilerParams(vmem_limit_bytes=VMEM_LIMIT),
        cost_estimate=pl.CostEstimate(
            flops=2 * 3 * 128 * 9216 * 256, bytes_accessed=40_000_000, transcendentals=0
        ),
    )(*operands)


def place_kernel(table_ref, new_ref, back_ref, out_ref, sem):
    rows = table_ref[2, 0]

    def send(k, carry):
        pltpu.make_async_copy(back_ref.at[table_ref[0, k]], out_ref.at[SLOTS + k], sem).start()
        return carry

    lax.fori_loop(0, rows, send, 0)

    def wait(k, carry):
        pltpu.make_async_copy(back_ref.at[0], out_ref.at[SLOTS], sem).wait()
        return carry

    lax.fori_loop(0, rows, wait, 0)


def place(table, new, back):
    hbm = pl.BlockSpec(memory_space=pl.ANY)
    vmem = pl.BlockSpec(memory_space=pltpu.VMEM)
    return pl.pallas_call(
        place_kernel,
        out_shape=jax.ShapeDtypeStruct(new.shape, F32),
        in_specs=[pl.BlockSpec(memory_space=pltpu.SMEM), hbm, vmem],
        out_specs=hbm,
        scratch_shapes=[pltpu.SemaphoreType.DMA],
        input_output_aliases={1: 0},
        compiler_params=pltpu.CompilerParams(vmem_limit_bytes=VMEM_LIMIT),
    )(table, new, back)


def nothing_kernel(x_ref, other_ref, out_ref):
    del x_ref, other_ref, out_ref


def after(x, other):
    hbm = pl.BlockSpec(memory_space=pl.ANY)
    return pl.pallas_call(
        nothing_kernel,
        out_shape=jax.ShapeDtypeStruct(x.shape, x.dtype),
        in_specs=[hbm, hbm],
        out_specs=hbm,
        input_output_aliases={0: 0},
    )(x, other)


def shards(amplitudes, hole_ladder, e_occ, e_vir, ladder_ints, pair_group):
    tile_cols = amplitudes.shape[1]
    capacity = 2 * pair_group.shape[0] // lax.axis_size("row")
    own = lax.axis_index("row")
    col_index = lax.axis_index("col")

    w_direct, w_mirror, slot_table, group_table, bin_table = prep(
        own.reshape(1), pair_group, e_occ, hole_ladder
    )
    w_direct = lax.all_gather(w_direct, "col", axis=0, tiled=True)
    w_mirror = lax.all_gather(w_mirror, "col", axis=0, tiled=True)
    mirror_hi, mirror_lo, direct_hi, direct_lo = tile_parts(amplitudes)

    direct = hole_product(False, w_direct, direct_hi, direct_lo)[0]
    direct = lax.all_to_all(direct, "row", 0, 0)
    tail_part, head_part = hole_product(True, w_mirror, mirror_hi, mirror_lo)

    def mirror_exchange(part, size):
        part = lax.all_to_all(part, "row", 0, 0).reshape(16, size, 640)
        return lax.all_to_all(part, "col", 0, 0)

    tail_mirror = mirror_exchange(after(tail_part, direct), TAIL)

    def own_slots(first, size):
        return lax.dynamic_slice(slot_table, (0, first + own * size), (2, size)).T

    tail_energy, head_energy = own_slots(0, TAIL), own_slots(BINS * TAIL, HEAD)
    local_energy = lax.dynamic_slice_in_dim(e_vir, col_index * tile_cols, tile_cols)
    virtual = e_vir.reshape(1, -1)
    counts, kept, taken = bin_table[:, 0], bin_table[:, 1], bin_table[:, 3]
    own_count = lax.dynamic_index_in_dim(counts, own, 0, False)
    own_kept = jnp.minimum(own_count, SLOTS)
    start = jnp.minimum(kept, SLOTS - SPILL)
    own_start = lax.dynamic_index_in_dim(start, own, 0, False)
    fits = (jnp.max(taken) <= SPILL) & jnp.all((taken == 0) | (kept >= HEAD))

    late_rows, late_part = combine(
        TAIL, local_energy, direct, tail_mirror, tail_energy, virtual, ladder_ints
    )
    head_mirror = mirror_exchange(after(head_part, late_part), HEAD)
    segment = lax.dynamic_slice_in_dim(late_rows, jnp.maximum(own_start - HEAD, 0), SPILL, 0)
    back = lax.all_gather(segment, "row", axis=0, tiled=True)

    def whole(meta, direct, head_mirror, late_rows):
        return combine(
            HEAD, local_energy, direct, head_mirror, head_energy, virtual, ladder_ints,
            (meta, late_rows, late_part), capacity,
        )

    new_rows, partial_value = whole(own_kept.reshape(1), direct, head_mirror, late_rows)

    blocks = lax.all_to_all(partial_value.reshape(16, 16, 128), "col", 0, 0)
    share = jnp.sum(blocks, axis=0)
    shares = lax.all_to_all(jnp.broadcast_to(share, (BINS, 16, 128)), "row", 0, 0)
    live = group_table[2, :capacity]
    from_bin, from_slot = group_table[0, :capacity], group_table[1, :capacity]
    where_from = jnp.where(live > 0, from_bin * 128 + from_slot, -1)
    pick = jnp.arange(BINS * 128, dtype=jnp.int32)[:, None] == where_from[None, :]
    ladder_share = jnp.dot(
        jnp.transpose(shares, (1, 0, 2)).reshape(16, BINS * 128),
        pick.astype(F32),
        precision=lax.Precision.HIGHEST,
        preferred_element_type=F32,
    )

    late_bin, late_slot = from_bin[SLOTS:], from_slot[SLOTS:]
    late_count = own_count - own_kept
    bin_start = jnp.sum(jnp.where(late_bin[:, None] == jnp.arange(BINS)[None, :], start[None, :], 0), axis=1)
    back_row = jnp.clip(late_bin * SPILL + late_slot - bin_start, 0, BINS * SPILL - 1)
    count_row = jnp.full_like(back_row, jnp.where(fits, late_count, 0))
    new_amps = place(jnp.stack([back_row, back_row, count_row]), new_rows, back)

    def long_way(carry):
        turn, new_amps, direct, head_mirror, late_rows = carry
        values, _ = whole(jnp.full((1,), SLOTS, jnp.int32) + turn, direct, head_mirror, late_rows)
        everything = lax.all_gather(values[:SLOTS], "row", axis=0, tiled=True)
        late = everything[late_bin * SLOTS + late_slot]
        rows = jnp.arange(capacity - SLOTS, dtype=jnp.int32)
        table = jnp.stack([rows, rows, jnp.full_like(rows, late_count)])
        return turn + 1, place(table, new_amps, late), direct, head_mirror, late_rows

    turns = jnp.where(fits, 0, 1)
    new_amps = lax.while_loop(
        lambda carry: carry[0] < turns, long_way, (jnp.int32(0), new_amps, direct, head_mirror, late_rows)
    )[1]
    return (new_amps[None], ladder_share[None])


def solution(mesh):
    return jax.shard_map(
        shards,
        mesh=mesh,
        in_specs=(P("row", "col", None), P("col", None), P(), P(), P("col", None, None), P()),
        out_specs=(P("row", None, "col", None), P("row", "col", None)),
        check_vma=False,
    )
```

time: 401 us -> 383 us (0.955)
  the two profiles are of different devices: /device:TPU:8 before, /device:TPU:0 now
where the time goes in v1:
time: 383 us; the launch traced here: 378 us
  waiting for transfers between devices  143 us (37%)
  Pallas kernels  108 us (28%)
  blocking collectives  75.2 us (20%)
  starting transfers between devices  23.4 us (6%)
  between operations  17.3 us (5%)
  local copies, waits for them, and re-layouts  7.24 us (2%)
    all_to_all x2, waiting for transfers between devices, mirror_exchange(): return lax.all_to_all(part, 'col', 0, 0)  78.2 us
    all_to_all x2, blocking collectives, mirror_exchange(): part = lax.all_to_all(part, 'row', 0, 0).reshape(16, size, 640)  75.2 us
    pallas_call x2, Pallas kernels, hole_product(): pl.pallas_call(functools.partial(hole_kernel, mirror), out_shape=tuple((j...  39.3 us
    pallas_call x1, Pallas kernels, tile_parts(): pl.pallas_call(tile_kernel, out_shape=(jax.ShapeDtypeStruct((1280, 1600),...  33.4 us
    all_gather x1, waiting for transfers between devices, shards(): w_mirror = lax.all_gather(w_mirror, 'col', axis=0, tiled=True)  31.4 us
    pallas_call x2, Pallas kernels, combine(): pl.pallas_call(functools.partial(combine_kernel, head is not None, size),...  22.5 us
    all_gather x1, waiting for transfers between devices, shards(): w_direct = lax.all_gather(w_direct, 'col', axis=0, tiled=True)  9.86 us
    all_to_all x1, waiting for transfers between devices, shards(): direct = lax.all_to_all(direct, 'row', 0, 0)  9.2 us
  transfers between devices with their start and end apart: 8, of which 7 were waited for; matrix products, arithmetic and copies ran while one was open for 1% of the time, Pallas kernels for 23%

profile of v1, /device:TPU:0, one launch (start us, length us, event | category | flops | bytes accessed | tf_op | source)
XLA Modules:
  0.0 377.9 jit_solution(18209076056367399813)
XLA Ops:
  7.2 0.7 pad.4
  8.5 1.3 copy.23.eocc_ref
  9.8 8.1 %shard_map.86 = (f32[104,832]{1,0:T(8,128)}, f32[104,832]{1,0:T(8,128)}, f32[8,832]{1,0:T(8,128)}, s32[8,256]{1,0:T(8,128)}, s32[8,128]{1,0:T(8,128)}) custom-call(s32[1]{0:T(128)} %bitcast.3.own_ref, s32[1,896]{1,0:T(1,128)} %reshape.89.group_ref, f32[8,896]{1,0:T(8,128)} %constant.79.clone.occ_ref, f32[40,1]{1,0:T(8,128)} %copy.23.eocc_ref, f32[100,1600]{1,0:T(8,128)} %w_ref.1), custom_call_target="tpu_custom_call" | custom-call | tf_op jit(solution)/shard_map/pallas_call | solution.py:125
  18.8 33.4 %shard_map.87 = (bf16[1280,1600]{1,0:T(8,128)(2,1)}, bf16[1280,1600]{1,0:T(8,128)(2,1)}, bf16[1280,1600]{1,0:T(8,128)(2,1)}, bf16[1280,1600]{1,0:T(8,128)(2,1)}) custom-call(f32[48,24,1600]{2,1,0:T(8,128)} %t_ref.1), custom_call_target="tpu_custom_call" | custom-call | bytes 60000000 | tf_op jit(solution)/shard_map/pallas_call | solution.py:165
  52.2 9.9 %all-gather.5.cloned.1.call-done.w_ref = f32[1664,832]{1,0:T(8,128)} async-done(((f32[104,832]{1,0:T(8,128)}), f32[1664,832]{1,0:T(8,128)}) %all-gather.5.cloned.1.call-update) | async-done | bytes 5537808 | tf_op jit(solution)/shard_map/all_gather | solution.py:376
  62.0 19.7 %shard_map.88 = f32[8,104,1152]{2,1,0:T(8,128)} custom-call(f32[1664,832]{1,0:T(8,128)} %all-gather.5.cloned.1.call-done.w_ref, bf16[1280,1600]{1,0:T(8,128)(2,1)} %get-tuple-element.94.t_hi, bf16[1280,1600]{1,0:T(8,128)(2,1)} %get-tuple-element.95.t_lo), custom_call_target="tpu_custom_call" | custom-call | flops 10223616000 | bytes 17000000 | tf_op jit(solution)/shard_map/pallas_call | solution.py:210
  81.8 6.4 %all-to-all-start = ((f32[8,104,1152]{2,1,0:T(8,128)}), f32[8,104,1152]{2,1,0:T(8,128)}, u32[]{:S(2)}, u32[]{:S(2)}) async-start(f32[8,104,1152]{2,1,0:T(8,128)} %shard_map.88), calls=%async_computation | async-start | bytes 7667712 | tf_op jit(solution)/shard_map/all_to_all | solution.py:381
  88.2 31.4 %all-gather.7.cloned.1.call-done.w_ref = f32[1664,832]{1,0:T(8,128)} async-done(((f32[104,832]{1,0:T(8,128)}), f32[1664,832]{1,0:T(8,128)}) %all-gather.7.cloned.1.call-update) | async-done | bytes 5537808 | tf_op jit(solution)/shard_map/all_gather | solution.py:377
  119.5 19.5 %shard_map.89 = (f32[8,2,32,640]{3,2,1,0:T(8,128)}, f32[8,2,72,640]{3,2,1,0:T(8,128)}) custom-call(f32[1664,832]{1,0:T(8,128)} %all-gather.7.cloned.1.call-done.w_ref, bf16[1280,1600]{1,0:T(8,128)(2,1)} %get-tuple-element.97.t_hi, bf16[1280,1600]{1,0:T(8,128)(2,1)} %get-tuple-element.98.t_lo), custom_call_target="tpu_custom_call" | custom-call | flops 10223616000 | bytes 17000000 | tf_op jit(solution)/shard_map/pallas_call | solution.py:210
  139.1 9.2 %all-to-all-done.other_ref.refs_1_.refs_2_ = f32[8,104,1152]{2,1,0:T(8,128)} async-done(((f32[8,104,1152]{2,1,0:T(8,128)}), f32[8,104,1152]{2,1,0:T(8,128)}, u32[]{:S(2)}, u32[]{:S(2)}) %all-to-all-start) | async-done | bytes 3833888 | tf_op jit(solution)/shard_map/all_to_all | solution.py:381
  148.3 24.6 %all_to_all.35 = f32[8,2,32,640]{3,2,1,0:T(8,128)} all-to-all(f32[8,2,32,640]{3,2,1,0:T(8,128)} %shard_map.90), channel_id=1, replica_groups=mesh['row'=8,'col'=16] {'row'}, dimensions={0} | all-to-all | bytes 2621440 | tf_op jit(solution)/shard_map/all_to_all | solution.py:385
  172.9 4.2 %all-to-all-start.2 = ((f32[16,32,640]{2,1,0:T(8,128)}), f32[16,32,640]{2,1,0:T(8,128)S(1)}, u32[]{:S(2)}, u32[]{:S(2)}) async-start(f32[16,32,640]{2,1,0:T(8,128)} %bitcast.9), calls=%async_computation.2 | async-start | bytes 2621440 | tf_op jit(solution)/shard_map/all_to_all | solution.py:386
  177.6 0.7 slice_minimum_fusion
  179.5 0.6 dynamic-slice_bitcast_fusion.1.refs_3_
  180.1 16.4 %all-to-all-done.2.refs_2_ = f32[16,32,640]{2,1,0:T(8,128)S(1)} async-done(((f32[16,32,640]{2,1,0:T(8,128)}), f32[16,32,640]{2,1,0:T(8,128)S(1)}, u32[]{:S(2)}, u32[]{:S(2)}) %all-to-all-start.2) | async-done | bytes 1310752 | tf_op jit(solution)/shard_map/all_to_all | solution.py:386
  196.5 1.1 copy-done.1
  197.6 8.8 %shard_map.91 = (f32[32,24,384]{2,1,0:T(8,128)S(1)}, f32[32,256]{1,0:T(8,128)S(1)}) custom-call(f32[24]{0:T(128)S(1)} %dynamic_slice.20.refs_0_.refs_1_, f32[8,104,1152]{2,1,0:T(8,128)} %all-to-all-done.other_ref.refs_1_.refs_2_, f32[16,32,640]{2,1,0:T(8,128)} %copy-done.1, f32[32,2]{1,0:T(8,128)} %dynamic-slice_bitcast_fusion.1.refs_3_, ...), custom_call_target="tpu_custom_call" | custom-call | flops 1811939328 | bytes 40000000 | tf_op jit(solution)/shard_map/pallas_call | solution.py:308
  206.4 1.0 copy-done
  207.4 0.9 constant_dynamic-slice_fusion
  208.3 50.6 %all_to_all.36 = f32[8,2,72,640]{3,2,1,0:T(8,128)} all-to-all(f32[8,2,72,640]{3,2,1,0:T(8,128)} %shard_map.92), channel_id=1, replica_groups=mesh['row'=8,'col'=16] {'row'}, dimensions={0} | all-to-all | bytes 5898240 | tf_op jit(solution)/shard_map/all_to_all | solution.py:385
  259.0 3.9 %all-to-all-start.4 = ((f32[16,72,640]{2,1,0:T(8,128)}), f32[16,72,640]{2,1,0:T(8,128)S(1)}, u32[]{:S(2)}, u32[]{:S(2)}) async-start(f32[16,72,640]{2,1,0:T(8,128)} %bitcast.48), calls=%async_computation.4 | async-start | bytes 5898240 | tf_op jit(solution)/shard_map/all_to_all | solution.py:386
  264.7 0.7 or_reduce_fusion
  266.3 61.8 %all-to-all-done.4.refs_3_ = f32[16,72,640]{2,1,0:T(8,128)S(1)} async-done(((f32[16,72,640]{2,1,0:T(8,128)}), f32[16,72,640]{2,1,0:T(8,128)S(1)}, u32[]{:S(2)}, u32[]{:S(2)}) %all-to-all-start.4) | async-done | bytes 2949152 | tf_op jit(solution)/shard_map/all_to_all | solution.py:386
  328.1 13.7 %shard_map.93 = (f32[205,24,384]{2,1,0:T(8,128)}, f32[256,128]{1,0:T(8,128)}) custom-call(s32[1]{0:T(128)} %bitcast.8.refs_0_, f32[24]{0:T(128)S(1)} %dynamic_slice.20.refs_0_.refs_1_, f32[8,104,1152]{2,1,0:T(8,128)} %all-to-all-done.other_ref.refs_1_.refs_2_, f32[16,72,640]{2,1,0:T(8,128)S(1)} %all-to-all-done.4.refs_3_, ...), custom_call_target="tpu_custom_call" | custom-call | flops 1811939328 | bytes 40000000 | tf_op jit(solution)/shard_map/pallas_call | solution.py:308
  341.8 3.5 all-to-all-start.5
  345.4 6.6 %all-to-all-done.5 = f32[16,16,128]{2,1,0:T(8,128)S(1)} async-done(((f32[16,16,128]{2,1,0:T(8,128)}), f32[16,16,128]{2,1,0:T(8,128)S(1)}, u32[]{:S(2)}, u32[]{:S(2)}) %all-to-all-start.5) | async-done | bytes 131104 | tf_op jit(solution)/shard_map/all_to_all | solution.py:418
  352.0 0.6 broadcast_in_dim.42
  352.6 4.9 %all-to-all-start.6 = ((f32[8,16,128]{2,1,0:T(8,128)}), f32[8,16,128]{2,1,0:T(8,128)S(1)}, u32[]{:S(2)}, u32[]{:S(2)}) async-start(f32[8,16,128]{2,1,0:T(8,128)} %broadcast_in_dim.42), calls=%async_computation.6 | async-start | bytes 131072 | tf_op jit(solution)/shard_map/all_to_all | solution.py:420
  357.6 0.6 add_add_fusion.1.table_ref
  358.2 7.2 %all-to-all-done.6 = f32[8,16,128]{2,1,0:T(8,128)S(1)} async-done(((f32[8,16,128]{2,1,0:T(8,128)}), f32[8,16,128]{2,1,0:T(8,128)S(1)}, u32[]{:S(2)}, u32[]{:S(2)}) %all-to-all-start.6) | async-done | bytes 65568 | tf_op jit(solution)/shard_map/all_to_all | solution.py:420
  365.4 1.0 convolution_bitcast_fusion
  366.5 4.4 %shard_map.94 = f32[205,24,384]{2,1,0:T(8,128)} custom-call(s32[3,101]{1,0:T(4,128)} %add_add_fusion.1.table_ref, f32[205,24,384]{2,1,0:T(8,128)} %get-tuple-element.104.new_ref, f32[144,24,384]{2,1,0:T(8,128)} %all-gather.9.cloned.1.call-done.back_ref), custom_call_target="tpu_custom_call", output_to_operand_aliasing={{}: (1, {})} | custom-call | tf_op jit(solution)/shard_map/pallas_call | solution.py:341
  (32 shorter events, 3.1 us)
Async XLA Ops:
  7.2 54.9 %all-gather.5.cloned.1.call-start = ((), (), s32[]{:S(2)}) async-start(), calls=%async_computation.7 | async-start | bytes 6336512 | tf_op jit(solution)/shard_map/all_gather | solution.py:376
  18.0 101.5 %all-gather.7.cloned.1.call-start = ((), (), s32[]{:S(2)}) async-start(), calls=%async_computation.8 | async-start | bytes 6336512 | tf_op jit(solution)/shard_map/all_gather | solution.py:377
  81.8 66.5 %all-to-all-start = ((f32[8,104,1152]{2,1,0:T(8,128)}), f32[8,104,1152]{2,1,0:T(8,128)}, u32[]{:S(2)}, u32[]{:S(2)}) async-start(f32[8,104,1152]{2,1,0:T(8,128)} %shard_map.88), calls=%async_computation | async-start | bytes 7667712 | tf_op jit(solution)/shard_map/all_to_all | solution.py:381
  148.3 29.1 %copy-start.4 = (f32[384]{0:T(512)S(1)}, f32[384]{0:T(512)}, u32[]{:S(2)}) copy-start(f32[384]{0:T(512)} %param.12) | copy-start | bytes 4612
  148.3 29.2 %copy-start.3 = (f32[8,832]{1,0:T(8,128)S(1)}, f32[8,832]{1,0:T(8,128)}, u32[]{:S(2)}) copy-start(f32[8,832]{1,0:T(8,128)} %get-tuple-element.101) | copy-start | bytes 79876
  148.3 29.3 %copy-start.2 = (s32[8,128]{1,0:T(8,128)S(1)}, s32[8,128]{1,0:T(8,128)}, u32[]{:S(2)}) copy-start(s32[8,128]{1,0:T(8,128)} %get-tuple-element.92) | copy-start | bytes 12292
  172.9 23.6 %all-to-all-start.2 = ((f32[16,32,640]{2,1,0:T(8,128)}), f32[16,32,640]{2,1,0:T(8,128)S(1)}, u32[]{:S(2)}, u32[]{:S(2)}) async-start(f32[16,32,640]{2,1,0:T(8,128)} %bitcast.9), calls=%async_computation.2 | async-start | bytes 2621440 | tf_op jit(solution)/shard_map/all_to_all | solution.py:386
  177.1 189.4 %all-gather.9.cloned.1.call-start = ((), (), s32[]{:S(2)}) async-start(), calls=%async_computation.9 | async-start | bytes 5971968 | tf_op jit(solution)/shard_map/all_gather | solution.py:408
  196.5 1.1 copy-start.1
  206.4 1.0 copy-start
  259.0 7.1 %copy-start.5 = (s32[8,256]{1,0:T(8,128)S(1)}, s32[8,256]{1,0:T(8,128)}, u32[]{:S(2)}) copy-start(s32[8,256]{1,0:T(8,128)} %get-tuple-element.91) | copy-start | bytes 24580
  259.0 69.1 %all-to-all-start.4 = ((f32[16,72,640]{2,1,0:T(8,128)}), f32[16,72,640]{2,1,0:T(8,128)S(1)}, u32[]{:S(2)}, u32[]{:S(2)}) async-start(f32[16,72,640]{2,1,0:T(8,128)} %bitcast.48), calls=%async_computation.4 | async-start | bytes 5898240 | tf_op jit(solution)/shard_map/all_to_all | solution.py:386
  341.8 10.2 %all-to-all-start.5 = ((f32[16,16,128]{2,1,0:T(8,128)}), f32[16,16,128]{2,1,0:T(8,128)S(1)}, u32[]{:S(2)}, u32[]{:S(2)}) async-start(f32[16,16,128]{2,1,0:T(8,128)} %bitcast.49), calls=%async_computation.5 | async-start | bytes 262144 | tf_op jit(solution)/shard_map/all_to_all | solution.py:418
  352.6 12.8 %all-to-all-start.6 = ((f32[8,16,128]{2,1,0:T(8,128)}), f32[8,16,128]{2,1,0:T(8,128)S(1)}, u32[]{:S(2)}, u32[]{:S(2)}) async-start(f32[8,16,128]{2,1,0:T(8,128)} %broadcast_in_dim.42), calls=%async_computation.6 | async-start | bytes 131072 | tf_op jit(solution)/shard_map/all_to_all | solution.py:420
Sparse Core Ops, SparseCore 0:
  18.1 43.8 all-gather.4
  63.7 55.7 all-gather.6
  208.5 127.9 all-gather.8

commit v2 on v1

--- a/solution.py
+++ b/solution.py
@@ -172,8 +172,7 @@
     )(amplitudes)
 
 
-def hole_kernel(mirror, w_ref, t_hi, t_lo, *refs):
-    out_refs, (wn, wt_hi, wt_lo) = refs[:-3], refs[-3:]
+def hole_kernel(mirror, w_ref, t_hi, t_lo, out_ref, wn, wt_hi, wt_lo):
     for s in range(16):
         wn[100 * s : 100 * s + 100, :] = w_ref[104 * s : 104 * s + 100, :]
     for lane in range(0, ALL_SLOTS, 128):
@@ -189,29 +188,27 @@
             for u in range(2):
                 h, lane = divmod(2 * n + u, 5)
                 first = 0
-                for out_ref, size in zip(out_refs, (TAIL, HEAD)):
+                for slots in (slice(HEAD, SLOTS), slice(0, HEAD)):
                     for b in range(BINS):
-                        out_ref[b, h, :, 128 * lane : 128 * (lane + 1)] = y[
-                            first : first + size, 128 * u : 128 * (u + 1)
+                        last = first + slots.stop - slots.start
+                        out_ref[b, h, slots, 128 * lane : 128 * (lane + 1)] = y[
+                            first:last, 128 * u : 128 * (u + 1)
                         ]
-                        first += size
+                        first = last
         else:
             wide = 256 if n < 4 else 128
             for b in range(BINS):
-                out_refs[0][b, :, 256 * n : 256 * n + wide] = y[SLOTS * b : SLOTS * (b + 1), 0:wide]
+                out_ref[b, :, 256 * n : 256 * n + wide] = y[SLOTS * b : SLOTS * (b + 1), 0:wide]
 
 
 def hole_product(mirror, gathered, hi, lo):
-    if mirror:
-        shapes = [(BINS, 2, TAIL, 640), (BINS, 2, HEAD, 640)]
-    else:
-        shapes = [(BINS, SLOTS, 1152)]
+    shape = (BINS, 2, SLOTS, 640) if mirror else (BINS, SLOTS, 1152)
     vmem = pl.BlockSpec(memory_space=pltpu.VMEM)
     return pl.pallas_call(
         functools.partial(hole_kernel, mirror),
-        out_shape=tuple(jax.ShapeDtypeStruct(shape, F32) for shape in shapes),
+        out_shape=jax.ShapeDtypeStruct(shape, F32),
         in_specs=[vmem] * 3,
-        out_specs=(vmem,) * len(shapes),
+        out_specs=vmem,
         scratch_shapes=[
             pltpu.VMEM((1600, ALL_SLOTS), F32),
             pltpu.VMEM((ALL_SLOTS, 1600), BF16),
@@ -377,15 +374,12 @@
     w_mirror = lax.all_gather(w_mirror, "col", axis=0, tiled=True)
     mirror_hi, mirror_lo, direct_hi, direct_lo = tile_parts(amplitudes)
 
-    direct = hole_product(False, w_direct, direct_hi, direct_lo)[0]
+    direct = hole_product(False, w_direct, direct_hi, direct_lo)
     direct = lax.all_to_all(direct, "row", 0, 0)
-    tail_part, head_part = hole_product(True, w_mirror, mirror_hi, mirror_lo)
-
-    def mirror_exchange(part, size):
-        part = lax.all_to_all(part, "row", 0, 0).reshape(16, size, 640)
-        return lax.all_to_all(part, "col", 0, 0)
-
-    tail_mirror = mirror_exchange(after(tail_part, direct), TAIL)
+    mirror = after(hole_product(True, w_mirror, mirror_hi, mirror_lo), direct)
+    mirror = lax.all_to_all(mirror, "row", 0, 0).reshape(16, SLOTS, 640)
+    tail_mirror = lax.all_to_all(mirror[:, HEAD:], "col", 0, 0)
+    head_mirror = lax.all_to_all(after(mirror[:, :HEAD], tail_mirror), "col", 0, 0)
 
     def own_slots(first, size):
         return lax.dynamic_slice(slot_table, (0, first + own * size), (2, size)).T
@@ -403,7 +397,6 @@
     late_rows, late_part = combine(
         TAIL, local_energy, direct, tail_mirror, tail_energy, virtual, ladder_ints
     )
-    head_mirror = mirror_exchange(after(head_part, late_part), HEAD)
     segment = lax.dynamic_slice_in_dim(late_rows, jnp.maximum(own_start - HEAD, 0), SPILL, 0)
     back = lax.all_gather(segment, "row", axis=0, tiled=True)
 

time: 383 us -> 353 us (0.922)
  blocking collectives: 75.2 us -> 55.5 us
  waiting for transfers between devices: 143 us -> 126 us
  local copies, waits for them, and re-layouts: 7.24 us -> 14.2 us
    all_to_all x2 -> x1, blocking collectives: 75.2 us -> 55.5 us  [shards(): mirror = lax.all_to_all(mirror, 'row', 0, 0).reshape(16, SLOTS, 640)]
    all_to_all x2, waiting for transfers between devices: 78.2 us -> 61 us  [the longest x1 44.6 us: shards(): lax.all_to_all(after(mirror[:, :HEAD], tail_mirror), 'col', 0, 0)]
    slice x0 -> x2, local copies, waits for them, and re-layouts: none -> 4.83 us  [the longest x1 3.62 us: shards(): mirror[:, :HEAD]]
  transfers between devices with their start and end apart: 8 -> 8, of which waited for: 7 -> 7; matrix products, arithmetic and copies ran while one was open for 1% -> 3% of each run, Pallas kernels for 23% -> 25%
where the time goes in v2:
time: 353 us; the launch traced here: 346 us
  waiting for transfers between devices  126 us (36%)
  Pallas kernels  106 us (30%)
  blocking collectives  55.5 us (16%)
  starting transfers between devices  23.6 us (7%)
  between operations  17.2 us (5%)
  local copies, waits for them, and re-layouts  14.2 us (4%)
    all_to_all x1, blocking collectives, shards(): mirror = lax.all_to_all(mirror, 'row', 0, 0).reshape(16, SLOTS, 640)  55.5 us
    all_to_all x1, waiting for transfers between devices, shards(): lax.all_to_all(after(mirror[:, :HEAD], tail_mirror), 'col', 0, 0)  44.6 us
    pallas_call x2, Pallas kernels, hole_product(): pl.pallas_call(functools.partial(hole_kernel, mirror), out_shape=jax.Shap...  39.4 us
    pallas_call x1, Pallas kernels, tile_parts(): pl.pallas_call(tile_kernel, out_shape=(jax.ShapeDtypeStruct((1280, 1600),...  33.4 us
    all_gather x1, waiting for transfers between devices, shards(): w_mirror = lax.all_gather(w_mirror, 'col', axis=0, tiled=True)  31.4 us
    pallas_call x2, Pallas kernels, combine(): pl.pallas_call(functools.partial(combine_kernel, head is not None, size),...  22.5 us
    all_to_all x1, waiting for transfers between devices, shards(): tail_mirror = lax.all_to_all(mirror[:, HEAD:], 'col', 0, 0)  16.4 us
    all_gather x1, waiting for transfers between devices, shards(): w_direct = lax.all_gather(w_direct, 'col', axis=0, tiled=True)  9.86 us
  transfers between devices with their start and end apart: 8, of which 7 were waited for; matrix products, arithmetic and copies ran while one was open for 3% of the time, Pallas kernels for 25%

profile of v2, /device:TPU:0, one launch (start us, length us, event | category | flops | bytes accessed | tf_op | source)
XLA Modules:
  0.0 346.3 jit_solution(12224273396430634686)
XLA Ops:
  7.2 0.7 pad.4
  8.5 1.3 copy.23.eocc_ref
  9.8 8.2 %shard_map.86 = (f32[104,832]{1,0:T(8,128)}, f32[104,832]{1,0:T(8,128)}, f32[8,832]{1,0:T(8,128)}, s32[8,256]{1,0:T(8,128)}, s32[8,128]{1,0:T(8,128)}) custom-call(s32[1]{0:T(128)} %bitcast.3.own_ref, s32[1,896]{1,0:T(1,128)} %reshape.86.group_ref, f32[8,896]{1,0:T(8,128)} %constant.79.clone.occ_ref, f32[40,1]{1,0:T(8,128)} %copy.23.eocc_ref, f32[100,1600]{1,0:T(8,128)} %w_ref.1), custom_call_target="tpu_custom_call" | custom-call | tf_op jit(solution)/shard_map/pallas_call | solution.py:125
  18.8 33.4 %shard_map.87 = (bf16[1280,1600]{1,0:T(8,128)(2,1)}, bf16[1280,1600]{1,0:T(8,128)(2,1)}, bf16[1280,1600]{1,0:T(8,128)(2,1)}, bf16[1280,1600]{1,0:T(8,128)(2,1)}) custom-call(f32[48,24,1600]{2,1,0:T(8,128)} %t_ref.1), custom_call_target="tpu_custom_call" | custom-call | bytes 60000000 | tf_op jit(solution)/shard_map/pallas_call | solution.py:165
  52.2 9.9 %all-gather.5.cloned.1.call-done.w_ref = f32[1664,832]{1,0:T(8,128)} async-done(((f32[104,832]{1,0:T(8,128)}), f32[1664,832]{1,0:T(8,128)}) %all-gather.5.cloned.1.call-update) | async-done | bytes 5537808 | tf_op jit(solution)/shard_map/all_gather | solution.py:373
  62.0 19.7 %shard_map.88 = f32[8,104,1152]{2,1,0:T(8,128)} custom-call(f32[1664,832]{1,0:T(8,128)} %all-gather.5.cloned.1.call-done.w_ref, bf16[1280,1600]{1,0:T(8,128)(2,1)} %get-tuple-element.92.t_hi, bf16[1280,1600]{1,0:T(8,128)(2,1)} %get-tuple-element.93.t_lo), custom_call_target="tpu_custom_call" | custom-call | flops 10223616000 | bytes 17000000 | tf_op jit(solution)/shard_map/pallas_call | solution.py:207
  81.8 6.4 %all-to-all-start = ((f32[8,104,1152]{2,1,0:T(8,128)}), f32[8,104,1152]{2,1,0:T(8,128)}, u32[]{:S(2)}, u32[]{:S(2)}) async-start(f32[8,104,1152]{2,1,0:T(8,128)} %shard_map.88), calls=%async_computation | async-start | bytes 7667712 | tf_op jit(solution)/shard_map/all_to_all | solution.py:378
  88.2 31.4 %all-gather.7.cloned.1.call-done.w_ref = f32[1664,832]{1,0:T(8,128)} async-done(((f32[104,832]{1,0:T(8,128)}), f32[1664,832]{1,0:T(8,128)}) %all-gather.7.cloned.1.call-update) | async-done | bytes 5537808 | tf_op jit(solution)/shard_map/all_gather | solution.py:374
  119.6 19.7 %shard_map.89.x_ref = f32[8,2,104,640]{3,2,1,0:T(8,128)} custom-call(f32[1664,832]{1,0:T(8,128)} %all-gather.7.cloned.1.call-done.w_ref, bf16[1280,1600]{1,0:T(8,128)(2,1)} %get-tuple-element.95.t_hi, bf16[1280,1600]{1,0:T(8,128)(2,1)} %get-tuple-element.96.t_lo), custom_call_target="tpu_custom_call" | custom-call | flops 10223616000 | bytes 17000000 | tf_op jit(solution)/shard_map/pallas_call | solution.py:207
  139.3 9.0 %all-to-all-done.other_ref.refs_1_.refs_2_ = f32[8,104,1152]{2,1,0:T(8,128)} async-done(((f32[8,104,1152]{2,1,0:T(8,128)}), f32[8,104,1152]{2,1,0:T(8,128)}, u32[]{:S(2)}, u32[]{:S(2)}) %all-to-all-start) | async-done | bytes 3833888 | tf_op jit(solution)/shard_map/all_to_all | solution.py:378
  148.3 55.5 %all_to_all.30 = f32[8,2,104,640]{3,2,1,0:T(8,128)S(1)} all-to-all(f32[8,2,104,640]{3,2,1,0:T(8,128)} %shard_map.90), channel_id=1, replica_groups=mesh['row'=8,'col'=16] {'row'}, dimensions={0} | all-to-all | bytes 8519680 | tf_op jit(solution)/shard_map/all_to_all | solution.py:380
  203.8 2.0 copy-done.1
  205.8 1.2 slice.53
  207.1 4.5 %all-to-all-start.2 = ((f32[16,32,640]{2,1,0:T(8,128)}), f32[16,32,640]{2,1,0:T(8,128)S(1)}, u32[]{:S(2)}, u32[]{:S(2)}) async-start(f32[16,32,640]{2,1,0:T(8,128)} %slice.53), calls=%async_computation.2 | async-start | bytes 2621440 | tf_op jit(solution)/shard_map/all_to_all | solution.py:381
  212.2 0.7 slice_minimum_fusion
  214.7 16.4 %all-to-all-done.2.other_ref.refs_2_ = f32[16,32,640]{2,1,0:T(8,128)S(1)} async-done(((f32[16,32,640]{2,1,0:T(8,128)}), f32[16,32,640]{2,1,0:T(8,128)S(1)}, u32[]{:S(2)}, u32[]{:S(2)}) %all-to-all-start.2) | async-done | bytes 1310752 | tf_op jit(solution)/shard_map/all_to_all | solution.py:381
  231.1 1.1 copy-done.2
  232.2 8.8 %shard_map.92 = (f32[32,24,384]{2,1,0:T(8,128)S(1)}, f32[32,256]{1,0:T(8,128)S(1)}) custom-call(f32[24]{0:T(128)S(1)} %dynamic_slice.20.refs_0_.refs_1_, f32[8,104,1152]{2,1,0:T(8,128)} %all-to-all-done.other_ref.refs_1_.refs_2_, f32[16,32,640]{2,1,0:T(8,128)} %copy-done.2, f32[32,2]{1,0:T(8,128)} %dynamic-slice_bitcast_fusion.1.refs_3_, ...), custom_call_target="tpu_custom_call" | custom-call | flops 1811939328 | bytes 40000000 | tf_op jit(solution)/shard_map/pallas_call | solution.py:305
  241.0 1.0 copy-done
  242.0 0.9 constant_dynamic-slice_fusion
  243.0 3.6 %slice.52.x_ref = f32[16,72,640]{2,1,0:T(8,128)} slice(f32[16,104,640]{2,1,0:T(8,128)} %bitcast.48), slice={[0:16], [0:72], [0:640]} | slice | bytes 5898240 | tf_op jit(solution)/shard_map/slice | solution.py:382
  246.6 3.9 %all-to-all-start.3 = ((f32[16,72,640]{2,1,0:T(8,128)}), f32[16,72,640]{2,1,0:T(8,128)S(1)}, u32[]{:S(2)}, u32[]{:S(2)}) async-start(f32[16,72,640]{2,1,0:T(8,128)} %shard_map.91), calls=%async_computation.3 | async-start | bytes 5898240 | tf_op jit(solution)/shard_map/all_to_all | solution.py:382
  252.3 0.7 or_reduce_fusion
  253.9 44.6 %all-to-all-done.3.refs_3_ = f32[16,72,640]{2,1,0:T(8,128)S(1)} async-done(((f32[16,72,640]{2,1,0:T(8,128)}), f32[16,72,640]{2,1,0:T(8,128)S(1)}, u32[]{:S(2)}, u32[]{:S(2)}) %all-to-all-start.3) | async-done | bytes 2949152 | tf_op jit(solution)/shard_map/all_to_all | solution.py:382
  298.5 13.7 %shard_map.93 = (f32[205,24,384]{2,1,0:T(8,128)}, f32[256,128]{1,0:T(8,128)}) custom-call(s32[1]{0:T(128)} %bitcast.8.refs_0_, f32[24]{0:T(128)S(1)} %dynamic_slice.20.refs_0_.refs_1_, f32[8,104,1152]{2,1,0:T(8,128)} %all-to-all-done.other_ref.refs_1_.refs_2_, f32[16,72,640]{2,1,0:T(8,128)S(1)} %all-to-all-done.3.refs_3_, ...), custom_call_target="tpu_custom_call" | custom-call | flops 1811939328 | bytes 40000000 | tf_op jit(solution)/shard_map/pallas_call | solution.py:305
  312.1 3.8 %all-to-all-start.4 = ((f32[16,16,128]{2,1,0:T(8,128)}), f32[16,16,128]{2,1,0:T(8,128)S(1)}, u32[]{:S(2)}, u32[]{:S(2)}) async-start(f32[16,16,128]{2,1,0:T(8,128)} %bitcast.49), calls=%async_computation.4 | async-start | bytes 262144 | tf_op jit(solution)/shard_map/all_to_all | solution.py:411
  316.0 6.7 %all-to-all-done.4 = f32[16,16,128]{2,1,0:T(8,128)S(1)} async-done(((f32[16,16,128]{2,1,0:T(8,128)}), f32[16,16,128]{2,1,0:T(8,128)S(1)}, u32[]{:S(2)}, u32[]{:S(2)}) %all-to-all-start.4) | async-done | bytes 131104 | tf_op jit(solution)/shard_map/all_to_all | solution.py:411
  323.3 4.5 %all-to-all-start.5 = ((f32[8,16,128]{2,1,0:T(8,128)}), f32[8,16,128]{2,1,0:T(8,128)S(1)}, u32[]{:S(2)}, u32[]{:S(2)}) async-start(f32[8,16,128]{2,1,0:T(8,128)} %broadcast_in_dim.42), calls=%async_computation.5 | async-start | bytes 131072 | tf_op jit(solution)/shard_map/all_to_all | solution.py:413
  327.8 0.6 add_add_fusion.1.table_ref
  328.5 7.2 %all-to-all-done.5 = f32[8,16,128]{2,1,0:T(8,128)S(1)} async-done(((f32[8,16,128]{2,1,0:T(8,128)}), f32[8,16,128]{2,1,0:T(8,128)S(1)}, u32[]{:S(2)}, u32[]{:S(2)}) %all-to-all-start.5) | async-done | bytes 65568 | tf_op jit(solution)/shard_map/all_to_all | solution.py:413
  335.7 1.0 convolution_bitcast_fusion
  336.7 2.5 shard_map.94
  (35 shorter events, 4.3 us)
Async XLA Ops:
  7.2 54.9 %all-gather.5.cloned.1.call-start = ((), (), s32[]{:S(2)}) async-start(), calls=%async_computation.6 | async-start | bytes 6336512 | tf_op jit(solution)/shard_map/all_gather | solution.py:373
  18.0 101.5 %all-gather.7.cloned.1.call-start = ((), (), s32[]{:S(2)}) async-start(), calls=%async_computation.7 | async-start | bytes 6336512 | tf_op jit(solution)/shard_map/all_gather | solution.py:374
  81.8 66.5 %all-to-all-start = ((f32[8,104,1152]{2,1,0:T(8,128)}), f32[8,104,1152]{2,1,0:T(8,128)}, u32[]{:S(2)}, u32[]{:S(2)}) async-start(f32[8,104,1152]{2,1,0:T(8,128)} %shard_map.88), calls=%async_computation | async-start | bytes 7667712 | tf_op jit(solution)/shard_map/all_to_all | solution.py:378
  203.8 2.0 copy-start.1
  203.8 8.1 %copy-start.5 = (f32[384]{0:T(512)S(1)}, f32[384]{0:T(512)}, u32[]{:S(2)}) copy-start(f32[384]{0:T(512)} %param.12) | copy-start | bytes 4612
  203.8 8.2 %copy-start.4 = (f32[8,832]{1,0:T(8,128)S(1)}, f32[8,832]{1,0:T(8,128)}, u32[]{:S(2)}) copy-start(f32[8,832]{1,0:T(8,128)} %get-tuple-element.97) | copy-start | bytes 79876
  203.8 8.3 %copy-start.3 = (s32[8,128]{1,0:T(8,128)S(1)}, s32[8,128]{1,0:T(8,128)}, u32[]{:S(2)}) copy-start(s32[8,128]{1,0:T(8,128)} %get-tuple-element.90) | copy-start | bytes 12292
  207.1 24.0 %all-to-all-start.2 = ((f32[16,32,640]{2,1,0:T(8,128)}), f32[16,32,640]{2,1,0:T(8,128)S(1)}, u32[]{:S(2)}, u32[]{:S(2)}) async-start(f32[16,32,640]{2,1,0:T(8,128)} %slice.53), calls=%async_computation.2 | async-start | bytes 2621440 | tf_op jit(solution)/shard_map/all_to_all | solution.py:381
  211.6 125.1 %all-gather.9.cloned.1.call-start = ((), (), s32[]{:S(2)}) async-start(), calls=%async_computation.8 | async-start | bytes 5971968 | tf_op jit(solution)/shard_map/all_gather | solution.py:401
  231.1 1.1 copy-start.2
  241.0 1.0 copy-start
  246.6 7.1 %copy-start.6 = (s32[8,256]{1,0:T(8,128)S(1)}, s32[8,256]{1,0:T(8,128)}, u32[]{:S(2)}) copy-start(s32[8,256]{1,0:T(8,128)} %get-tuple-element.89) | copy-start | bytes 24580
  246.6 51.9 %all-to-all-start.3 = ((f32[16,72,640]{2,1,0:T(8,128)}), f32[16,72,640]{2,1,0:T(8,128)S(1)}, u32[]{:S(2)}, u32[]{:S(2)}) async-start(f32[16,72,640]{2,1,0:T(8,128)} %shard_map.91), calls=%async_computation.3 | async-start | bytes 5898240 | tf_op jit(solution)/shard_map/all_to_all | solution.py:382
  312.1 10.5 %all-to-all-start.4 = ((f32[16,16,128]{2,1,0:T(8,128)}), f32[16,16,128]{2,1,0:T(8,128)S(1)}, u32[]{:S(2)}, u32[]{:S(2)}) async-start(f32[16,16,128]{2,1,0:T(8,128)} %bitcast.49), calls=%async_computation.4 | async-start | bytes 262144 | tf_op jit(solution)/shard_map/all_to_all | solution.py:411
  323.3 12.4 %all-to-all-start.5 = ((f32[8,16,128]{2,1,0:T(8,128)}), f32[8,16,128]{2,1,0:T(8,128)S(1)}, u32[]{:S(2)}, u32[]{:S(2)}) async-start(f32[8,16,128]{2,1,0:T(8,128)} %broadcast_in_dim.42), calls=%async_computation.5 | async-start | bytes 131072 | tf_op jit(solution)/shard_map/all_to_all | solution.py:413
Sparse Core Ops, SparseCore 0:
  18.1 43.8 all-gather.4
  63.7 55.7 all-gather.6
  243.1 90.0 all-gather.8

commit v3 on v2

--- a/solution.py
+++ b/solution.py
@@ -71,13 +71,15 @@
     bin_of = jnp.sum(bin_hot * bin_row.astype(F32), axis=0, keepdims=True)
     moved = jnp.sum(inside * (kept - first), axis=0, keepdims=True) + order[0:1, :]
     slot_of = jnp.where(is_spilled, moved, rank)
-    in_order = bin_of * float(SLOTS) + slot_of
+    in_bin = bin_of * float(SLOTS) + jnp.where(
+        slot_of >= float(HEAD), slot_of - float(HEAD), slot_of + float(TAIL)
+    )
     tail_first = jnp.where(
         slot_of >= float(HEAD),
         bin_of * float(TAIL) + slot_of - float(HEAD),
         bin_of * float(HEAD) + slot_of + float(BINS * TAIL),
     )
-    places = [jnp.where(valid > 0.5, place, -1.0) for place in (in_order, tail_first)]
+    places = [jnp.where(valid > 0.5, place, -1.0) for place in (in_bin, tail_first)]
     own_rank = jnp.where(group == own_ref[0], rank, -1.0)
     stack = jnp.concatenate(places + [own_rank, jnp.zeros((5, PAIR_PAD), F32)], axis=0)
     columns = jnp.transpose(stack, (1, 0)).astype(jnp.int32)
@@ -223,15 +225,14 @@
 
 def combine_kernel(head, size, *refs):
     if head:
-        meta_ref, ed_ref, d_ref, s_ref, eo_ref, ev_ref, ladder_ref, tail_ref, more_ref = refs[:9]
+        meta_ref, ed_ref, d_ref, s_ref, eo_ref, ev_ref, ladder_ref, tail_ref, flat_ref = refs[:9]
         new_ref, part_ref, m_ref, raw, acc = refs[9:]
     else:
-        ed_ref, d_ref, s_ref, eo_ref, ev_ref, ladder_ref = refs[:6]
-        raw, part_ref, m_ref, acc = refs[6:]
+        ed_ref, d_ref, s_ref, eo_ref, ev_ref, raw, m_ref = refs
     step = pl.program_id(0)
     energy = eo_ref[:, 0:1] - ev_ref[...]
     live = eo_ref[:, 1:2] > 0.5
-    rows = slice(0, size) if head else slice(SLOTS - size, SLOTS)
+    rows = slice(TAIL, SLOTS) if head else slice(0, TAIL)
 
     def group(j):
         for u in range(8):
@@ -240,19 +241,21 @@
             lane = 128 * (d // 5) + 24 * (d % 5)
             mirrored = jnp.concatenate([s_ref[c, :, lane : lane + 24] for c in range(16)], axis=1)
             value = jnp.where(live, (direct + mirrored) / (energy - ed_ref[d]), 0.0)
-            m_ref[:, 384 * u : 384 * (u + 1)] = value
+            m_ref[0:size, 384 * u : 384 * (u + 1)] = value
             raw[:, u, :] = value
 
     for j in range(3):
         pl.when(step == j)(functools.partial(group, j))
 
-    if head:
-        kept = meta_ref[0]
-        new_ref[0:size] = jnp.where(iota((size, 8, 384), 0) < kept, raw[...], 0.0)
-        tail = iota((SLOTS - size, 8, 384), 0) + size
-        new_ref[size:SLOTS] = jnp.where(tail < kept, tail_ref[...], 0.0)
-        new_ref[SLOTS:] = jnp.zeros((new_ref.shape[0] - SLOTS, 8, 384), F32)
-
+    if not head:
+        return
+    kept = meta_ref[0]
+    new_ref[0:size] = jnp.where(iota((size, 8, 384), 0) < kept, raw[...], 0.0)
+    tail = iota((SLOTS - size, 8, 384), 0) + size
+    new_ref[size:SLOTS] = jnp.where(tail < kept, tail_ref[...], 0.0)
+    new_ref[SLOTS:] = jnp.zeros((new_ref.shape[0] - SLOTS, 8, 384), F32)
+
+    m_ref[size:SLOTS, :] = flat_ref[...]
     left_hi, left_lo = split2(m_ref[...])
     right_hi, right_lo = split2(ladder_ref[...].reshape(8 * 384, 256))
     term = (dot(left_lo, right_hi) + dot(left_hi, right_lo)) + dot(left_hi, right_hi)
@@ -260,48 +263,49 @@
     @pl.when(step == 0)
     def _():
         acc[...] = jnp.zeros(acc.shape, F32)
-        if head:
-            acc[size:SLOTS, :] = more_ref[...]
-
-    acc[0:size, :] += term
+
+    acc[0:SLOTS, :] += term
 
     @pl.when(step == 2)
     def _():
-        part_ref[...] = jnp.transpose(acc[...], (1, 0)) if head else acc[...]
+        part_ref[...] = jnp.transpose(acc[...], (1, 0))
 
 
 def combine(size, ed, direct, mirrored, energy, ev, ladder, head=None, rows=0):
     smem = pl.BlockSpec(memory_space=pltpu.SMEM)
     in_specs = [
         smem,
-        pl.BlockSpec((8, SLOTS, 384), lambda j: (0, 0, j)),
+        pl.BlockSpec((8, TAIL if head is None else SLOTS, 384), lambda j: (0, 0, j)),
         pl.BlockSpec((16, size, 640), lambda j: (0, 0, 0)),
         pl.BlockSpec((size, 2), lambda j: (0, 0)),
         pl.BlockSpec((1, 384), lambda j: (0, 0)),
-        pl.BlockSpec((8, 384, 256), lambda j: (j, 0, 0)),
     ]
-    operands = [ed, direct, mirrored, energy, ev, ladder]
-    scratch = [pltpu.VMEM((size, 8 * 384), F32)]
+    operands = [ed, direct, mirrored, energy, ev]
+    scratch = []
     if head is None:
-        out_shape = (jax.ShapeDtypeStruct((size, 24, 384), F32), jax.ShapeDtypeStruct((size, 256), F32))
+        out_shape = (jax.ShapeDtypeStruct((size, 24, 384), F32), jax.ShapeDtypeStruct((size, 24 * 384), F32))
         out_specs = (
             pl.BlockSpec((size, 8, 384), lambda j: (0, j, 0)),
-            pl.BlockSpec((size, 256), lambda j: (0, 0)),
+            pl.BlockSpec((size, 8 * 384), lambda j: (0, j)),
         )
-        scratch += [pltpu.VMEM((size, 256), F32)]
     else:
-        meta, tail, more = head
-        operands = [meta] + operands + [tail, more]
+        meta, tail, flat = head
+        operands = [meta] + operands + [ladder, tail, flat]
         in_specs = [smem] + in_specs + [
+            pl.BlockSpec((8, 384, 256), lambda j: (j, 0, 0)),
             pl.BlockSpec((SLOTS - size, 8, 384), lambda j: (0, j, 0)),
-            pl.BlockSpec((SLOTS - size, 256), lambda j: (0, 0)),
+            pl.BlockSpec((SLOTS - size, 8 * 384), lambda j: (0, j)),
         ]
         out_shape = (jax.ShapeDtypeStruct((rows, 24, 384), F32), jax.ShapeDtypeStruct((256, 128), F32))
         out_specs = (
             pl.BlockSpec((rows, 8, 384), lambda j: (0, j, 0)),
             pl.BlockSpec((256, 128), lambda j: (0, 0)),
         )
-        scratch += [pltpu.VMEM((size, 8, 384), F32), pltpu.VMEM((128, 256), F32)]
+        scratch += [
+            pltpu.VMEM((SLOTS, 8 * 384), F32),
+            pltpu.VMEM((size, 8, 384), F32),
+            pltpu.VMEM((128, 256), F32),
+        ]
     return pl.pallas_call(
         functools.partial(combine_kernel, head is not None, size),
         grid=(3,),
@@ -394,7 +398,7 @@
     own_start = lax.dynamic_index_in_dim(start, own, 0, False)
     fits = (jnp.max(taken) <= SPILL) & jnp.all((taken == 0) | (kept >= HEAD))
 
-    late_rows, late_part = combine(
+    late_rows, late_flat = combine(
         TAIL, local_energy, direct, tail_mirror, tail_energy, virtual, ladder_ints
     )
     segment = lax.dynamic_slice_in_dim(late_rows, jnp.maximum(own_start - HEAD, 0), SPILL, 0)
@@ -403,7 +407,7 @@
     def whole(meta, direct, head_mirror, late_rows):
         return combine(
             HEAD, local_energy, direct, head_mirror, head_energy, virtual, ladder_ints,
-            (meta, late_rows, late_part), capacity,
+            (meta, late_rows, late_flat), capacity,
         )
 
     new_rows, partial_value = whole(own_kept.reshape(1), direct, head_mirror, late_rows)

time: 353 us -> 349 us (0.989)
  no operation moved by 1% of the time
where the time goes in v3:
time: 349 us; the launch traced here: 343 us
  waiting for transfers between devices  125 us (36%)
  Pallas kernels  103 us (30%)
  blocking collectives  55.5 us (16%)
  starting transfers between devices  23.6 us (7%)
  between operations  17.3 us (5%)
  local copies, waits for them, and re-layouts  14.2 us (4%)
    all_to_all x1, blocking collectives, shards(): mirror = lax.all_to_all(mirror, 'row', 0, 0).reshape(16, SLOTS, 640)  55.5 us
    all_to_all x1, waiting for transfers between devices, shards(): lax.all_to_all(after(mirror[:, :HEAD], tail_mirror), 'col', 0, 0)  44.5 us
    pallas_call x2, Pallas kernels, hole_product(): pl.pallas_call(functools.partial(hole_kernel, mirror), out_shape=jax.Shap...  39.4 us
    pallas_call x1, Pallas kernels, tile_parts(): pl.pallas_call(tile_kernel, out_shape=(jax.ShapeDtypeStruct((1280, 1600),...  33.4 us
    all_gather x1, waiting for transfers between devices, shards(): w_mirror = lax.all_gather(w_mirror, 'col', axis=0, tiled=True)  31.4 us
    pallas_call x2, Pallas kernels, combine(): pl.pallas_call(functools.partial(combine_kernel, head is not None, size),...  19.2 us
    all_to_all x1, waiting for transfers between devices, shards(): tail_mirror = lax.all_to_all(mirror[:, HEAD:], 'col', 0, 0)  16.3 us
    all_gather x1, waiting for transfers between devices, shards(): w_direct = lax.all_gather(w_direct, 'col', axis=0, tiled=True)  9.87 us
  transfers between devices with their start and end apart: 8, of which 7 were waited for; matrix products, arithmetic and copies ran while one was open for 3% of the time, Pallas kernels for 25%

profile of v3, /device:TPU:0, one launch (start us, length us, event | category | flops | bytes accessed | tf_op | source)
XLA Modules:
  0.0 343.1 jit_solution(5496501917286689093)
XLA Ops:
  7.2 0.7 pad.4
  8.5 1.3 copy.23.eocc_ref
  9.8 8.1 %shard_map.86 = (f32[104,832]{1,0:T(8,128)}, f32[104,832]{1,0:T(8,128)}, f32[8,832]{1,0:T(8,128)}, s32[8,256]{1,0:T(8,128)}, s32[8,128]{1,0:T(8,128)}) custom-call(s32[1]{0:T(128)} %bitcast.3.own_ref, s32[1,896]{1,0:T(1,128)} %reshape.86.group_ref, f32[8,896]{1,0:T(8,128)} %constant.79.clone.occ_ref, f32[40,1]{1,0:T(8,128)} %copy.23.eocc_ref, f32[100,1600]{1,0:T(8,128)} %w_ref.1), custom_call_target="tpu_custom_call" | custom-call | tf_op jit(solution)/shard_map/pallas_call | solution.py:127
  18.8 33.4 %shard_map.87 = (bf16[1280,1600]{1,0:T(8,128)(2,1)}, bf16[1280,1600]{1,0:T(8,128)(2,1)}, bf16[1280,1600]{1,0:T(8,128)(2,1)}, bf16[1280,1600]{1,0:T(8,128)(2,1)}) custom-call(f32[48,24,1600]{2,1,0:T(8,128)} %t_ref.1), custom_call_target="tpu_custom_call" | custom-call | bytes 60000000 | tf_op jit(solution)/shard_map/pallas_call | solution.py:167
  52.2 9.9 %all-gather.5.cloned.1.call-done.w_ref = f32[1664,832]{1,0:T(8,128)} async-done(((f32[104,832]{1,0:T(8,128)}), f32[1664,832]{1,0:T(8,128)}) %all-gather.5.cloned.1.call-update) | async-done | bytes 5537808 | tf_op jit(solution)/shard_map/all_gather | solution.py:377
  62.0 19.7 %shard_map.88 = f32[8,104,1152]{2,1,0:T(8,128)} custom-call(f32[1664,832]{1,0:T(8,128)} %all-gather.5.cloned.1.call-done.w_ref, bf16[1280,1600]{1,0:T(8,128)(2,1)} %get-tuple-element.92.t_hi, bf16[1280,1600]{1,0:T(8,128)(2,1)} %get-tuple-element.93.t_lo), custom_call_target="tpu_custom_call" | custom-call | flops 10223616000 | bytes 17000000 | tf_op jit(solution)/shard_map/pallas_call | solution.py:209
  81.8 6.4 %all-to-all-start = ((f32[8,104,1152]{2,1,0:T(8,128)}), f32[8,104,1152]{2,1,0:T(8,128)}, u32[]{:S(2)}, u32[]{:S(2)}) async-start(f32[8,104,1152]{2,1,0:T(8,128)} %shard_map.88), calls=%async_computation | async-start | bytes 7667712 | tf_op jit(solution)/shard_map/all_to_all | solution.py:382
  88.2 31.4 %all-gather.7.cloned.1.call-done.w_ref = f32[1664,832]{1,0:T(8,128)} async-done(((f32[104,832]{1,0:T(8,128)}), f32[1664,832]{1,0:T(8,128)}) %all-gather.7.cloned.1.call-update) | async-done | bytes 5537808 | tf_op jit(solution)/shard_map/all_gather | solution.py:378
  119.6 19.7 %shard_map.89.x_ref = f32[8,2,104,640]{3,2,1,0:T(8,128)} custom-call(f32[1664,832]{1,0:T(8,128)} %all-gather.7.cloned.1.call-done.w_ref, bf16[1280,1600]{1,0:T(8,128)(2,1)} %get-tuple-element.95.t_hi, bf16[1280,1600]{1,0:T(8,128)(2,1)} %get-tuple-element.96.t_lo), custom_call_target="tpu_custom_call" | custom-call | flops 10223616000 | bytes 17000000 | tf_op jit(solution)/shard_map/pallas_call | solution.py:209
  139.2 9.0 %all-to-all-done.other_ref.refs_1_.refs_2_ = f32[8,104,1152]{2,1,0:T(8,128)} async-done(((f32[8,104,1152]{2,1,0:T(8,128)}), f32[8,104,1152]{2,1,0:T(8,128)}, u32[]{:S(2)}, u32[]{:S(2)}) %all-to-all-start) | async-done | bytes 3833888 | tf_op jit(solution)/shard_map/all_to_all | solution.py:382
  148.3 55.5 %all_to_all.30 = f32[8,2,104,640]{3,2,1,0:T(8,128)S(1)} all-to-all(f32[8,2,104,640]{3,2,1,0:T(8,128)} %shard_map.90), channel_id=1, replica_groups=mesh['row'=8,'col'=16] {'row'}, dimensions={0} | all-to-all | bytes 8519680 | tf_op jit(solution)/shard_map/all_to_all | solution.py:384
  203.8 2.0 copy-done.1
  205.9 1.2 slice.53
  207.1 4.5 %all-to-all-start.2 = ((f32[16,32,640]{2,1,0:T(8,128)}), f32[16,32,640]{2,1,0:T(8,128)S(1)}, u32[]{:S(2)}, u32[]{:S(2)}) async-start(f32[16,32,640]{2,1,0:T(8,128)} %slice.53), calls=%async_computation.2 | async-start | bytes 2621440 | tf_op jit(solution)/shard_map/all_to_all | solution.py:385
  212.2 0.8 slice_minimum_fusion
  214.8 16.3 %all-to-all-done.2.other_ref.refs_2_ = f32[16,32,640]{2,1,0:T(8,128)S(1)} async-done(((f32[16,32,640]{2,1,0:T(8,128)}), f32[16,32,640]{2,1,0:T(8,128)S(1)}, u32[]{:S(2)}, u32[]{:S(2)}) %all-to-all-start.2) | async-done | bytes 1310752 | tf_op jit(solution)/shard_map/all_to_all | solution.py:385
  231.1 1.1 copy-done.2
  232.2 5.4 %shard_map.92 = (f32[32,24,384]{2,1,0:T(8,128)S(1)}, f32[32,9216]{1,0:T(8,128)}) custom-call(f32[24]{0:T(128)S(1)} %dynamic_slice.20.refs_0_.refs_1_, f32[8,104,1152]{2,1,0:T(8,128)} %all-to-all-done.other_ref.refs_1_.refs_2_, f32[16,32,640]{2,1,0:T(8,128)} %copy-done.2, f32[32,2]{1,0:T(8,128)} %dynamic-slice_bitcast_fusion.1.refs_3_, ...), custom_call_target="tpu_custom_call" | custom-call | flops 1811939328 | bytes 40000000 | tf_op jit(solution)/shard_map/pallas_call | solution.py:309
  237.6 1.0 copy-done
  238.7 0.9 constant_dynamic-slice_fusion
  239.6 3.6 %slice.52.x_ref = f32[16,72,640]{2,1,0:T(8,128)} slice(f32[16,104,640]{2,1,0:T(8,128)} %bitcast.48), slice={[0:16], [0:72], [0:640]} | slice | bytes 5898240 | tf_op jit(solution)/shard_map/slice | solution.py:386
  243.2 3.9 %all-to-all-start.3 = ((f32[16,72,640]{2,1,0:T(8,128)}), f32[16,72,640]{2,1,0:T(8,128)S(1)}, u32[]{:S(2)}, u32[]{:S(2)}) async-start(f32[16,72,640]{2,1,0:T(8,128)} %shard_map.91), calls=%async_computation.3 | async-start | bytes 5898240 | tf_op jit(solution)/shard_map/all_to_all | solution.py:386
  249.0 0.7 or_reduce_fusion
  250.6 44.5 %all-to-all-done.3.refs_3_ = f32[16,72,640]{2,1,0:T(8,128)S(1)} async-done(((f32[16,72,640]{2,1,0:T(8,128)}), f32[16,72,640]{2,1,0:T(8,128)S(1)}, u32[]{:S(2)}, u32[]{:S(2)}) %all-to-all-start.3) | async-done | bytes 2949152 | tf_op jit(solution)/shard_map/all_to_all | solution.py:386
  295.1 13.8 %shard_map.93 = (f32[205,24,384]{2,1,0:T(8,128)}, f32[256,128]{1,0:T(8,128)}) custom-call(s32[1]{0:T(128)} %bitcast.8.refs_0_, f32[24]{0:T(128)S(1)} %dynamic_slice.20.refs_0_.refs_1_, f32[8,104,1152]{2,1,0:T(8,128)} %all-to-all-done.other_ref.refs_1_.refs_2_, f32[16,72,640]{2,1,0:T(8,128)S(1)} %all-to-all-done.3.refs_3_, ...), custom_call_target="tpu_custom_call" | custom-call | flops 1811939328 | bytes 40000000 | tf_op jit(solution)/shard_map/pallas_call | solution.py:309
  308.9 3.7 %all-to-all-start.4 = ((f32[16,16,128]{2,1,0:T(8,128)}), f32[16,16,128]{2,1,0:T(8,128)S(1)}, u32[]{:S(2)}, u32[]{:S(2)}) async-start(f32[16,16,128]{2,1,0:T(8,128)} %bitcast.49), calls=%async_computation.4 | async-start | bytes 262144 | tf_op jit(solution)/shard_map/all_to_all | solution.py:415
  312.7 6.6 %all-to-all-done.4 = f32[16,16,128]{2,1,0:T(8,128)S(1)} async-done(((f32[16,16,128]{2,1,0:T(8,128)}), f32[16,16,128]{2,1,0:T(8,128)S(1)}, u32[]{:S(2)}, u32[]{:S(2)}) %all-to-all-start.4) | async-done | bytes 131104 | tf_op jit(solution)/shard_map/all_to_all | solution.py:415
  320.0 4.6 %all-to-all-start.5 = ((f32[8,16,128]{2,1,0:T(8,128)}), f32[8,16,128]{2,1,0:T(8,128)S(1)}, u32[]{:S(2)}, u32[]{:S(2)}) async-start(f32[8,16,128]{2,1,0:T(8,128)} %broadcast_in_dim.42), calls=%async_computation.5 | async-start | bytes 131072 | tf_op jit(solution)/shard_map/all_to_all | solution.py:417
  324.5 0.6 add_add_fusion.1.table_ref
  325.2 7.2 %all-to-all-done.5 = f32[8,16,128]{2,1,0:T(8,128)S(1)} async-done(((f32[8,16,128]{2,1,0:T(8,128)}), f32[8,16,128]{2,1,0:T(8,128)S(1)}, u32[]{:S(2)}, u32[]{:S(2)}) %all-to-all-start.5) | async-done | bytes 65568 | tf_op jit(solution)/shard_map/all_to_all | solution.py:417
  332.4 1.0 convolution_bitcast_fusion
  333.4 2.5 shard_map.94
  (35 shorter events, 4.3 us)
Async XLA Ops:
  7.2 54.9 %all-gather.5.cloned.1.call-start = ((), (), s32[]{:S(2)}) async-start(), calls=%async_computation.6 | async-start | bytes 6336512 | tf_op jit(solution)/shard_map/all_gather | solution.py:377
  18.0 101.5 %all-gather.7.cloned.1.call-start = ((), (), s32[]{:S(2)}) async-start(), calls=%async_computation.7 | async-start | bytes 6336512 | tf_op jit(solution)/shard_map/all_gather | solution.py:378
  81.8 66.5 %all-to-all-start = ((f32[8,104,1152]{2,1,0:T(8,128)}), f32[8,104,1152]{2,1,0:T(8,128)}, u32[]{:S(2)}, u32[]{:S(2)}) async-start(f32[8,104,1152]{2,1,0:T(8,128)} %shard_map.88), calls=%async_computation | async-start | bytes 7667712 | tf_op jit(solution)/shard_map/all_to_all | solution.py:382
  203.8 2.0 copy-start.1
  203.8 8.0 %copy-start.5 = (f32[384]{0:T(512)S(1)}, f32[384]{0:T(512)}, u32[]{:S(2)}) copy-start(f32[384]{0:T(512)} %param.12) | copy-start | bytes 4612
  203.8 8.1 %copy-start.4 = (f32[8,832]{1,0:T(8,128)S(1)}, f32[8,832]{1,0:T(8,128)}, u32[]{:S(2)}) copy-start(f32[8,832]{1,0:T(8,128)} %get-tuple-element.97) | copy-start | bytes 79876
  203.8 8.3 %copy-start.3 = (s32[8,128]{1,0:T(8,128)S(1)}, s32[8,128]{1,0:T(8,128)}, u32[]{:S(2)}) copy-start(s32[8,128]{1,0:T(8,128)} %get-tuple-element.90) | copy-start | bytes 12292
  207.1 24.0 %all-to-all-start.2 = ((f32[16,32,640]{2,1,0:T(8,128)}), f32[16,32,640]{2,1,0:T(8,128)S(1)}, u32[]{:S(2)}, u32[]{:S(2)}) async-start(f32[16,32,640]{2,1,0:T(8,128)} %slice.53), calls=%async_computation.2 | async-start | bytes 2621440 | tf_op jit(solution)/shard_map/all_to_all | solution.py:385
  211.6 121.8 %all-gather.9.cloned.1.call-start = ((), (), s32[]{:S(2)}) async-start(), calls=%async_computation.8 | async-start | bytes 5971968 | tf_op jit(solution)/shard_map/all_gather | solution.py:405
  231.1 1.1 copy-start.2
  237.6 1.0 copy-start
  243.2 7.2 %copy-start.6 = (s32[8,256]{1,0:T(8,128)S(1)}, s32[8,256]{1,0:T(8,128)}, u32[]{:S(2)}) copy-start(s32[8,256]{1,0:T(8,128)} %get-tuple-element.89) | copy-start | bytes 24580
  243.2 51.9 %all-to-all-start.3 = ((f32[16,72,640]{2,1,0:T(8,128)}), f32[16,72,640]{2,1,0:T(8,128)S(1)}, u32[]{:S(2)}, u32[]{:S(2)}) async-start(f32[16,72,640]{2,1,0:T(8,128)} %shard_map.91), calls=%async_computation.3 | async-start | bytes 5898240 | tf_op jit(solution)/shard_map/all_to_all | solution.py:386
  308.9 10.4 %all-to-all-start.4 = ((f32[16,16,128]{2,1,0:T(8,128)}), f32[16,16,128]{2,1,0:T(8,128)S(1)}, u32[]{:S(2)}, u32[]{:S(2)}) async-start(f32[16,16,128]{2,1,0:T(8,128)} %bitcast.49), calls=%async_computation.4 | async-start | bytes 262144 | tf_op jit(solution)/shard_map/all_to_all | solution.py:415
  320.0 12.4 %all-to-all-start.5 = ((f32[8,16,128]{2,1,0:T(8,128)}), f32[8,16,128]{2,1,0:T(8,128)S(1)}, u32[]{:S(2)}, u32[]{:S(2)}) async-start(f32[8,16,128]{2,1,0:T(8,128)} %broadcast_in_dim.42), calls=%async_computation.5 | async-start | bytes 131072 | tf_op jit(solution)/shard_map/all_to_all | solution.py:417
Sparse Core Ops, SparseCore 0:
  18.1 43.8 all-gather.4
  63.7 55.7 all-gather.6
  239.7 89.9 all-gather.8
